TPU v7x, 512 devices: a whole 4x8x8 slice. The times are simulated.
512 devices in a mesh: tm: 16 (over x, z_lo), space: 32 (over z_hi, y, core).
Axes of the slice: x: 4, y: 8, z: 8 (z_hi: 2, z_lo: 4; z = z_hi * 4 + z_lo), core: 2. Of those that a mesh axis runs over, the one named last changes fastest.
Arguments:
- volumes: bfloat16 [16, 1024, 4096], P('tm', 'space'), may hold values from -4 to 4
- shifts: int32 [2, 3, 16, 32], P(None, None, 'tm', 'space'), may hold values from -16 to 16
Outputs:
- correlations: float32 [2, 16, 32, 512], P(None, 'tm', 'space')
- registered: bfloat16 [16, 1024, 4096], P('tm', 'space')
- template: float32 [1024, 4096], P('space', 'tm')
All inputs are finite; a program needn't handle non-finite values.
Results may differ from a plain program's by a relative error of at most 0.02.
Values may be sent and summed in bfloat16 or wider, within the bound.
A program may use at most 64 MiB of HBM per device.

v0:
```python
import math

import jax
import jax.numpy as jnp
from jax import lax
from jax.sharding import PartitionSpec as P

PL = 64
TX = 32
LAGS = 8
ITERS = 2
HALO = 16


def extended(cells, sides, width):
    for axis, dim in sides:
        count = lax.axis_size(axis)
        ends = count - 1
        head = lax.slice_in_dim(cells, 0, width, axis=dim)
        tail = lax.slice_in_dim(cells, cells.shape[dim] - width, cells.shape[dim], axis=dim)
        cells = jnp.concatenate(
            [
                lax.ppermute(tail, axis, [(i, (i + 1) % count) for i in range(ends)]),
                cells,
                lax.ppermute(head, axis, [((i + 1) % count, i) for i in range(ends)]),
            ],
            axis=dim,
        )
    return cells


def dft_tables(length, lag_count):
    frequency = jnp.arange(length, dtype=jnp.int32)
    phases = frequency[:, None] * frequency[None, :] % length
    angles = phases.astype(jnp.float32) * (2.0 * math.pi / length)
    cosine = jnp.cos(angles)
    sine_tab = jnp.sin(angles)
    t_first = jnp.concatenate([cosine, -sine_tab], axis=0).astype(jnp.bfloat16)
    t_next = jnp.concatenate(
        [jnp.concatenate([cosine, sine_tab], axis=1), jnp.concatenate([-sine_tab, cosine], axis=1)],
        axis=0,
    ).astype(jnp.bfloat16)
    lag_steps = jnp.arange(lag_count, dtype=jnp.int32) - lag_count // 2
    lag_phase = lag_steps[:, None] * frequency[None, :] % length
    lag_angles = lag_phase.astype(jnp.float32) * (2.0 * math.pi / length)
    lag_cos = jnp.cos(lag_angles)
    lag_sin = jnp.sin(lag_angles)
    inv_pair = jnp.concatenate(
        [jnp.concatenate([lag_cos, -lag_sin], axis=1), jnp.concatenate([lag_sin, lag_cos], axis=1)],
        axis=0,
    ).astype(jnp.bfloat16)
    inv_real = jnp.concatenate([lag_cos, -lag_sin], axis=1).astype(jnp.bfloat16)
    return (t_first, t_next, inv_pair, inv_real)


def rotate_axes(array, stacked, leading, middle, trailing):
    return (
        array.reshape(stacked, leading, middle, trailing)
        .transpose(0, 2, 3, 1)
        .reshape(stacked * middle, trailing * leading)
    )


def first_section(t_first, patch_rows):
    return jnp.dot(t_first, patch_rows, preferred_element_type=jnp.float32).astype(jnp.bfloat16)


def later_sections(t_next, first_pass):
    length = first_pass.shape[0] // 2
    second = rotate_axes(first_pass, 2, length, length, length)
    third = rotate_axes(
        jnp.dot(t_next, second, preferred_element_type=jnp.float32).astype(jnp.bfloat16),
        2,
        length,
        length,
        length,
    )
    return rotate_axes(
        jnp.dot(t_next, third, preferred_element_type=jnp.float32).astype(jnp.bfloat16),
        2,
        length,
        length,
        length,
    )


def cross_spectrum(raw_spec, template_spec):
    length = raw_spec.shape[0] // 2
    raw_re = raw_spec[:length].astype(jnp.float32)
    raw_im = raw_spec[length:].astype(jnp.float32)
    tem_re = template_spec[:length].astype(jnp.float32)
    tem_im = template_spec[length:].astype(jnp.float32)
    return jnp.concatenate(
        [raw_re * tem_re + raw_im * tem_im, raw_im * tem_re - raw_re * tem_im], axis=0
    ).astype(jnp.bfloat16)


def lag_values(inv_pair, inv_real, crossed, lag_count):
    length = crossed.shape[0] // 2
    along_x = rotate_axes(
        jnp.dot(inv_pair, crossed, preferred_element_type=jnp.float32).astype(jnp.bfloat16),
        2,
        lag_count,
        length,
        length,
    )
    along_y = rotate_axes(
        jnp.dot(inv_pair, along_x, preferred_element_type=jnp.float32).astype(jnp.bfloat16),
        2,
        lag_count,
        length,
        lag_count,
    )
    along_z = jnp.dot(inv_real, along_y, preferred_element_type=jnp.float32)
    ordered = rotate_axes(along_z, 1, lag_count, lag_count, lag_count)
    return ordered.reshape(-1) * (1.0 / float(length) ** 6)


def warp_matrix(shift_one, n_out, n_in, offset):
    whole_cells = shift_one // 4
    fraction = (shift_one - 4 * whole_cells).astype(jnp.float32) * 0.25
    rows_idx = lax.broadcasted_iota(jnp.int32, (n_out, n_in), 0)
    cols_idx = lax.broadcasted_iota(jnp.int32, (n_out, n_in), 1)
    target = rows_idx + (offset - whole_cells)
    upper_weight = jnp.where(cols_idx == target, 1.0 - fraction, 0.0)
    lower_weight = jnp.where(cols_idx == target - 1, fraction, 0.0)
    return (upper_weight + lower_weight).astype(jnp.bfloat16)


def warp_patch(patch_rows, shift_vec, tile, length):
    across = warp_matrix(shift_vec[0], tile, length, (length - tile) // 2)
    shifted = (
        jnp.dot(across, patch_rows, preferred_element_type=jnp.float32)
        .astype(jnp.bfloat16)
        .reshape(tile, length, length)
    )
    second_mat = warp_matrix(shift_vec[1], length, length, 0)
    shifted = jnp.einsum(
        "iy,xyz->xiz", second_mat, shifted, preferred_element_type=jnp.float32
    ).astype(jnp.bfloat16)
    third_mat = warp_matrix(shift_vec[2], length, length, 0)
    shifted = jnp.einsum(
        "iz,xyz->xyi", third_mat, shifted, preferred_element_type=jnp.float32
    ).astype(jnp.bfloat16)
    return shifted.reshape(tile, length * length)


def on_device(volumes, shifts):
    vol_count = volumes.shape[0]
    total_vols = vol_count * lax.axis_size("tm")
    share_cols = volumes.shape[2] // lax.axis_size("tm")
    t_first, t_next, inv_pair, inv_real = dft_tables(PL, LAGS)
    padded = extended(volumes, (("space", 1),), HALO)
    raw_specs = later_sections(t_next, first_section(t_first, padded[0]))
    current = volumes
    results = []
    template_tile = None
    for iteration in range(ITERS):
        partial_value = jnp.sum(current.astype(jnp.float32), axis=0)
        mean_tile = (
            lax.psum(partial_value.astype(jnp.bfloat16), "tm").astype(jnp.float32) / total_vols
        )
        template_tile = lax.dynamic_slice_in_dim(
            mean_tile, lax.axis_index("tm") * share_cols, share_cols, 1
        )
        rimmed = extended(mean_tile.astype(jnp.bfloat16), (("space", 0),), HALO)
        first_pass = first_section(t_first, rimmed)
        template_spec = later_sections(t_next, first_pass)
        results.append(
            jnp.stack(
                [lag_values(inv_pair, inv_real, cross_spectrum(raw_specs, template_spec), LAGS)]
            )
        )
        current = jnp.stack([warp_patch(padded[0], shifts[iteration, :, 0, 0], TX, PL)])
    correlations = jnp.stack(results)[:, :, None, :]
    return (correlations, current, template_tile)


def solution(mesh):
    in_specs = (P("tm", "space", None), P(None, None, "tm", "space"))
    out_specs = (P(None, "tm", "space", None), P("tm", "space", None), P("space", "tm"))
    return jax.shard_map(
        on_device, mesh=mesh, in_specs=in_specs, out_specs=out_specs, check_vma=False
    )
```

profile of v0, /device:TPU:57, one launch (start us, length us, event | category | flops | bytes accessed | tf_op | source)
XLA Modules:
  0.0 338.6 jit_solution(8763226155924553445)
XLA Ops:
  8.2 10.4 %collective-permute-start = (bf16[1,16,4096]{2,1,0:T(8,128)(2,1)S(1)}, bf16[1,16,4096]{2,1,0:T(8,128)(2,1)S(1)}, u32[]{:S(2)}, u32[]{:S(2)}) collective-permute-start(bf16[1,16,4096]{2,1,0:T(8,128)(2,1)S(1)} %get-tuple-element.20), channel_id=1, source_target_pairs={{0,1},{1,2},{2,3},{3,4},{4,5},{5,6},{6,7},{7,8},{8,9},{9,10},{10,1... | collective-permute-start | bytes 393224 | tf_op jit(solution)/shard_map/ppermute | solution.py:23
  54.3 3.3 reshape.199
  63.3 3.3 reshape.201
  67.1 3.2 reshape.202
  70.3 3.3 copy.7
  73.6 140.7 %all-reduce.3.cloned.1.call-done = (bf16[32,4096]{1,0:T(8,128)(2,1)}, bf16[32,4096]{1,0:T(8,128)(2,1)}) async-done(((bf16[32,4096]{1,0:T(8,128)(2,1)}, bf16[32,4096]{1,0:T(8,128)(2,1)}), (bf16[32,4096]{1,0:T(8,128)(2,1)}, bf16[32,4096]{1,0:T(8,128)(2,1)})) %all-reduce.3.cloned.1.call-update) | async-done | bytes 524304 | tf_op jit(solution)/shard_map/psum | solution.py:161
  216.4 17.0 %collective-permute-start.4 = (bf16[16,4096]{1,0:T(8,128)(2,1)S(1)}, bf16[16,4096]{1,0:T(8,128)(2,1)S(1)}, u32[]{:S(2)}, u32[]{:S(2)}) collective-permute-start(bf16[16,4096]{1,0:T(8,128)(2,1)S(1)} %get-tuple-element.18), channel_id=1, source_target_pairs={{0,1},{1,2},{2,3},{3,4},{4,5},{5,6},{6,7},{7,8},{8,9},{9,10},{10,1... | collective-permute-start | bytes 393224 | tf_op jit(solution)/shard_map/ppermute | solution.py:23
  236.0 9.6 %collective-permute-start.2 = (bf16[16,4096]{1,0:T(8,128)(2,1)}, bf16[16,4096]{1,0:T(8,128)(2,1)}, u32[]{:S(2)}, u32[]{:S(2)}) collective-permute-start(bf16[16,4096]{1,0:T(8,128)(2,1)} %get-tuple-element.16), channel_id=1, source_target_pairs={{0,1},{1,2},{2,3},{3,4},{4,5},{5,6},{6,7},{7,8},{8,9},{9,10},{10,1... | collective-permute-start | bytes 393224 | tf_op jit(solution)/shard_map/ppermute | solution.py:23
  248.9 3.2 reshape.213
  252.2 4.2 %copy.14 = bf16[2,64,64,64]{1,3,2,0:T(8,128)(2,1)} copy(bf16[2,64,64,64]{3,2,1,0:T(8,128)(2,1)} %reshape.213) | data formatting | bytes 2097152 | tf_op jit(solution)/shard_map/reshape | solution.py:58
  256.3 3.3 reshape.214
  261.0 4.2 %reshape.215 = bf16[2,64,64,64]{3,2,1,0:T(8,128)(2,1)} reshape(bf16[128,4096]{1,0:T(8,128)(2,1)} %convolution_convert_fusion.1) | data formatting | bytes 2097152 | tf_op jit(solution)/shard_map/reshape | solution.py:58
  265.3 4.2 %copy.15 = bf16[2,64,64,64]{1,3,2,0:T(8,128)(2,1)} copy(bf16[2,64,64,64]{3,2,1,0:T(8,128)(2,1)} %reshape.215) | data formatting | bytes 2097152 | tf_op jit(solution)/shard_map/reshape | solution.py:58
  269.4 3.3 reshape.216
  274.2 4.2 %reshape.217 = bf16[2,64,64,64]{3,2,1,0:T(8,128)(2,1)} reshape(bf16[128,4096]{1,0:T(8,128)(2,1)} %convolution_convert_fusion) | data formatting | bytes 2097152 | tf_op jit(solution)/shard_map/reshape | solution.py:58
  278.4 4.2 %copy.16 = bf16[2,64,64,64]{1,3,2,0:T(8,128)(2,1)} copy(bf16[2,64,64,64]{3,2,1,0:T(8,128)(2,1)} %reshape.217) | data formatting | bytes 2097152 | tf_op jit(solution)/shard_map/reshape | solution.py:58
  287.2 4.2 %copy.8 = bf16[2,64,64,64]{1,3,2,0:T(8,128)(2,1)} copy(bf16[2,64,64,64]{3,2,1,0:T(8,128)(2,1)} %reshape.203) | data formatting | bytes 2097152 | tf_op jit(solution)/shard_map/reshape | solution.py:58
  291.4 3.3 reshape.204
  296.2 4.2 %reshape.205 = bf16[2,64,64,64]{3,2,1,0:T(8,128)(2,1)} reshape(bf16[128,4096]{1,0:T(8,128)(2,1)} %convolution_convert_fusion.4) | data formatting | bytes 2097152 | tf_op jit(solution)/shard_map/reshape | solution.py:58
  300.4 4.2 %copy.9 = bf16[2,64,64,64]{1,3,2,0:T(8,128)(2,1)} copy(bf16[2,64,64,64]{3,2,1,0:T(8,128)(2,1)} %reshape.205) | data formatting | bytes 2097152 | tf_op jit(solution)/shard_map/reshape | solution.py:58
  304.6 3.3 reshape.206
  309.3 4.2 %reshape.207 = bf16[2,64,64,64]{3,2,1,0:T(8,128)(2,1)} reshape(bf16[128,4096]{1,0:T(8,128)(2,1)} %convolution_convert_fusion.3) | data formatting | bytes 2097152 | tf_op jit(solution)/shard_map/reshape | solution.py:58
  313.5 4.2 %copy.10 = bf16[2,64,64,64]{1,3,2,0:T(8,128)(2,1)} copy(bf16[2,64,64,64]{3,2,1,0:T(8,128)(2,1)} %reshape.207) | data formatting | bytes 2097152 | tf_op jit(solution)/shard_map/reshape | solution.py:58
  317.7 4.6 %fusion.1 = (bf16[1,64,64,64]{3,2,1,0:T(8,128)(2,1)}, bf16[1,64,64,64]{3,2,1,0:T(8,128)(2,1)}, bf16[1,64,64,64]{3,2,1,0:T(8,128)(2,1)}, bf16[1,64,64,64]{3,2,1,0:T(8,128)(2,1)S(1)}) fusion(bf16[2,64,64,64]{3,2,1,0:T(8,128)(2,1)} %bitcast.124, bf16[2,64,64,64]{3,2,1,0:T(8,128)(2,1)S(1)} %bitcast.122, bf16[2,64,64,64]{3,2,1,0:T(8,128)(2,1)} %bitcast.123), kind=kLoop, calls=%fused_computation.22 | loop fusion | flops 5767168 | bytes 5242880 | tf_op jit(solution)/shard_map/convert.7
  (86 shorter events, 50.6 us)
Async XLA Ops:
  8.2 34.2 %collective-permute-start = (bf16[1,16,4096]{2,1,0:T(8,128)(2,1)S(1)}, bf16[1,16,4096]{2,1,0:T(8,128)(2,1)S(1)}, u32[]{:S(2)}, u32[]{:S(2)}) collective-permute-start(bf16[1,16,4096]{2,1,0:T(8,128)(2,1)S(1)} %get-tuple-element.20), channel_id=1, source_target_pairs={{0,1},{1,2},{2,3},{3,4},{4,5},{5,6},{6,7},{7,8},{8,9},{9,10},{10,1... | collective-permute-start | bytes 393224 | tf_op jit(solution)/shard_map/ppermute | solution.py:23
  18.6 23.8 %collective-permute-start.1 = (bf16[1,16,4096]{2,1,0:T(8,128)(2,1)S(1)}, bf16[1,16,4096]{2,1,0:T(8,128)(2,1)S(1)}, u32[]{:S(2)}, u32[]{:S(2)}) collective-permute-start(bf16[1,16,4096]{2,1,0:T(8,128)(2,1)S(1)} %get-tuple-element.21), channel_id=1, source_target_pairs={{1,0},{2,1},{3,2},{4,3},{5,4},{6,5},{7,6},{8,7},{9,8},{10,9},{11,1... | collective-permute-start | bytes 393224 | tf_op jit(solution)/shard_map/ppermute | solution.py:25
  38.2 7.7 %copy-start.2 = (bf16[1,32,4096]{2,1,0:T(8,128)(2,1)S(1)}, bf16[1,32,4096]{2,1,0:T(8,128)(2,1)}, u32[]{:S(2)}) copy-start(bf16[1,32,4096]{2,1,0:T(8,128)(2,1)} %param.2) | copy-start | bytes 786436
  48.8 165.6 %all-reduce.3.cloned.1.call-start = ((), (), s32[]{:S(2)}) async-start(), calls=%async_computation | async-start | bytes 1048576 | tf_op jit(solution)/shard_map/psum | solution.py:161
  216.4 32.1 %collective-permute-start.4 = (bf16[16,4096]{1,0:T(8,128)(2,1)S(1)}, bf16[16,4096]{1,0:T(8,128)(2,1)S(1)}, u32[]{:S(2)}, u32[]{:S(2)}) collective-permute-start(bf16[16,4096]{1,0:T(8,128)(2,1)S(1)} %get-tuple-element.18), channel_id=1, source_target_pairs={{0,1},{1,2},{2,3},{3,4},{4,5},{5,6},{6,7},{7,8},{8,9},{9,10},{10,1... | collective-permute-start | bytes 393224 | tf_op jit(solution)/shard_map/ppermute | solution.py:23
  233.4 15.1 %collective-permute-start.5 = (bf16[16,4096]{1,0:T(8,128)(2,1)S(1)}, bf16[16,4096]{1,0:T(8,128)(2,1)S(1)}, u32[]{:S(2)}, u32[]{:S(2)}) collective-permute-start(bf16[16,4096]{1,0:T(8,128)(2,1)S(1)} %get-tuple-element.19), channel_id=1, source_target_pairs={{1,0},{2,1},{3,2},{4,3},{5,4},{6,5},{7,6},{8,7},{9,8},{10,9},{11,1... | collective-permute-start | bytes 393224 | tf_op jit(solution)/shard_map/ppermute | solution.py:25
  236.0 46.5 %collective-permute-start.2 = (bf16[16,4096]{1,0:T(8,128)(2,1)}, bf16[16,4096]{1,0:T(8,128)(2,1)}, u32[]{:S(2)}, u32[]{:S(2)}) collective-permute-start(bf16[16,4096]{1,0:T(8,128)(2,1)} %get-tuple-element.16), channel_id=1, source_target_pairs={{0,1},{1,2},{2,3},{3,4},{4,5},{5,6},{6,7},{7,8},{8,9},{9,10},{10,1... | collective-permute-start | bytes 393224 | tf_op jit(solution)/shard_map/ppermute | solution.py:23
  245.7 36.9 %collective-permute-start.3 = (bf16[16,4096]{1,0:T(8,128)(2,1)}, bf16[16,4096]{1,0:T(8,128)(2,1)}, u32[]{:S(2)}, u32[]{:S(2)}) collective-permute-start(bf16[16,4096]{1,0:T(8,128)(2,1)} %get-tuple-element.17), channel_id=1, source_target_pairs={{1,0},{2,1},{3,2},{4,3},{5,4},{6,5},{7,6},{8,7},{9,8},{10,9},{11,1... | collective-permute-start | bytes 393224 | tf_op jit(solution)/shard_map/ppermute | solution.py:25
  322.3 2.2 copy-start.1
  325.3 2.1 copy-start
Sparse Core Ops, SparseCore 0:
  57.8 156.5 all-reduce.2
where the time goes:
time: 340 us; the launch traced here: 339 us
  waiting for transfers between devices  141 us (41%)
  local copies, waits for them, and re-layouts  100 us (29%)
  starting transfers between devices  43.2 us (13%)
  between operations  34 us (10%)
  matrix products  12.6 us (4%)
  other arithmetic  7.92 us (2%)
    psum x1, waiting for transfers between devices, on_device(): lax.psum(partial_value.astype(jnp.bfloat16), 'tm').astype(jnp.float32)  141 us
    reshape x24, local copies, waits for them, and re-layouts, rotate_axes(): array.reshape(stacked, leading, middle, trailing).transpose(0, 2, 3, 1)  67.2 us
    ppermute x3, starting transfers between devices, extended(): lax.ppermute(tail, axis, [(i, (i + 1) % count) for i in range(ends)])  37 us
    reshape x10, local copies, waits for them, and re-layouts, rotate_axes(): return array.reshape(stacked, leading, middle, trailing).transpose(0, 2,...  20.3 us
  transfers between devices with their start and end apart: 7, of which 1 were waited for; matrix products, arithmetic and copies ran while one was open for 16% of the time, Pallas kernels for 0%

commit v1 on v0

v1 whole, which is shorter than its diff:
```python
import functools

import jax
import jax.numpy as jnp
from jax import lax
from jax.experimental import pallas as pl
from jax.experimental.pallas import tpu as pltpu
from jax.sharding import PartitionSpec as P

MESH = pl.DeviceIdType.MESH
F32, BF16, I32 = jnp.float32, jnp.bfloat16, jnp.int32

PL = 64
TX = 32
HALO = 16
NT = 16
COLS = 256
SIDES = tuple((dt, ds) for ds in (-1, 1, 0) for dt in (-1, 0, 1) if (dt, ds) != (0, 0))


def band(shift, delta):
    whole = jnp.right_shift(shift, 2)
    fraction = (shift - 4 * whole).astype(F32) * 0.25
    return jnp.where(
        delta == whole, 1.0 - fraction, jnp.where(delta == whole + 1, fraction, 0.0)
    )


def kernel(
    ns, vol_ref, shift_ref, corr_ref, reg_ref, tmpl_ref,
    patch, raw, across, planes, xw, cur, got, win, turned, rolled, lagged, part, gath,
    local_sem, halo_send, halo_recv, raw_send, raw_recv, rim_send, rim_recv,
    cur_send, cur_recv, win_send, win_recv, part_send, part_recv,
):
    t = lax.axis_index("tm")
    s = lax.axis_index("space")
    has_lo, has_hi = s > 0, s < ns - 1
    there = {-1: has_lo, 1: has_hi}
    from_side = {-1: has_hi, 1: has_lo}

    def across_tm(k):
        return lax.rem(t + k + NT, NT)

    def each_peer(body):
        def step(k, carry):
            body(k)
            return carry

        lax.fori_loop(1, NT, step, 0)

    def remote(src, dst, send, recv, peer):
        return pltpu.make_async_remote_copy(
            src_ref=src, dst_ref=dst, send_sem=send, recv_sem=recv,
            device_id=peer, device_id_type=MESH,
        )

    own = pltpu.make_async_copy(vol_ref.at[0], patch.at[pl.ds(HALO, TX)], local_sem)
    own.start()

    barrier = pltpu.get_barrier_semaphore()
    each_peer(
        lambda k: pl.semaphore_signal(
            barrier, inc=1, device_id=(across_tm(k), s), device_id_type=MESH
        )
    )
    for ds in (-1, 1):

        @pl.when(there[ds])
        def _():
            for dt in (-1, 0, 1):
                pl.semaphore_signal(
                    barrier, inc=1, device_id=(across_tm(dt), s + ds), device_id_type=MESH
                )

    row = lax.broadcasted_iota(I32, (TX, PL), 0)
    col = lax.broadcasted_iota(I32, (TX, PL), 1)
    a = lax.broadcasted_iota(I32, (COLS, COLS), 0)
    b = lax.broadcasted_iota(I32, (COLS, COLS), 1)
    for i in range(2):
        across[i] = band(shift_ref[i, 0, 0, 0], row + HALO - col).astype(BF16)
        third = band(shift_ref[i, 2, 0, 0], (b & 63) - (a & 63))
        for d in range(4):
            second = band(shift_ref[i, 1, 0, 0], (b >> 6) - (a >> 6) - 4 * (d - 2))
            planes[i, d] = (second * third).astype(BF16)
    xw[0:64] = jnp.zeros((64, COLS), BF16)
    xw[18 * TX : 19 * TX] = jnp.zeros((TX, COLS), BF16)
    for ds, at in ((-1, 0), (1, 48)):

        @pl.when(jnp.logical_not(there[ds]))
        def _():
            patch[at : at + HALO] = jnp.zeros((HALO, PL * PL), BF16)
            raw[:, at : at + HALO] = jnp.zeros((NT, HALO, COLS), BF16)
            win[:, :, at : at + HALO] = jnp.zeros((2, 3, HALO, COLS), BF16)

    own.wait()
    pl.semaphore_wait(barrier, NT - 1 + 3 * (has_lo.astype(I32) + has_hi.astype(I32)))

    def halo(ds):
        src, dst = (HALO, 48) if ds < 0 else (TX, 0)
        k = 0 if ds < 0 else 1
        return remote(
            patch.at[pl.ds(src, HALO)], patch.at[pl.ds(dst, HALO)],
            halo_send.at[k], halo_recv.at[k], (t, s + ds),
        )

    def raw_copy(k):
        to = across_tm(k)
        return remote(
            patch.at[pl.ds(HALO, TX), pl.ds(pl.multiple_of(to * COLS, COLS), COLS)],
            raw.at[t, pl.ds(HALO, TX)],
            raw_send.at[k], raw_recv.at[k], (to, s),
        )

    for ds in (-1, 1):
        pl.when(there[ds])(halo(ds).start)
    each_peer(lambda k: raw_copy(k).start())
    raw[t, HALO : HALO + TX] = patch[
        HALO : HALO + TX, pl.ds(pl.multiple_of(t * COLS, COLS), COLS)
    ]
    for ds in (-1, 1):
        pl.when(from_side[ds])(halo(ds).wait_recv)

    def warp(i):
        for c in range(NT):
            xw[(c + 2) * TX : (c + 3) * TX] = jnp.dot(
                across[i], patch[:, c * COLS : (c + 1) * COLS], preferred_element_type=F32
            ).astype(BF16)
        total = jnp.dot(xw[0 : NT * TX], planes[i, 0], preferred_element_type=F32)
        for d in range(1, 4):
            total += jnp.dot(
                xw[d * TX : (d + NT) * TX], planes[i, d], preferred_element_type=F32
            )
        return total.astype(BF16)

    cur[...] = warp(0).reshape(NT, TX, COLS)

    def cur_copy(k):
        to = across_tm(k)
        return remote(cur.at[to], got.at[t], cur_send.at[k], cur_recv.at[k], (to, s))

    each_peer(lambda k: cur_copy(k).start())
    got[t] = cur[t]

    def win_copy(i, side, act):
        dt, ds = SIDES[side]
        src = {0: HALO, -1: HALO, 1: TX}[ds]
        dst = {0: HALO, -1: 48, 1: 0}[ds]
        rows = TX if ds == 0 else HALO
        copy = remote(
            win.at[i, 1, pl.ds(src, rows)], win.at[i, 1 - dt, pl.ds(dst, rows)],
            win_send.at[i, side], win_recv.at[i, side], (across_tm(dt), s + ds),
        )
        present = (from_side if act == "wait_recv" else there).get(ds)
        if present is None:
            getattr(copy, act)()
        else:
            pl.when(present)(getattr(copy, act))

    def windows(i, mean):
        win[i, 1, HALO : HALO + TX] = mean.astype(BF16)
        for side in range(8):
            win_copy(i, side, "start")

    each_peer(lambda k: raw_copy(k).wait_recv())
    windows(0, jnp.sum(raw[:, HALO : HALO + TX].astype(F32), axis=0) * (1.0 / NT))

    def rim(ds):
        src, dst = (HALO, 48) if ds < 0 else (TX, 0)
        k = 0 if ds < 0 else 1
        return remote(
            raw.at[:, pl.ds(src, HALO)], raw.at[:, pl.ds(dst, HALO)],
            rim_send.at[k], rim_recv.at[k], (t, s + ds),
        )

    for ds in (-1, 1):
        pl.when(there[ds])(rim(ds).start)

    moved = warp(1)
    for c in range(NT):
        reg_ref[0, :, c * COLS : (c + 1) * COLS] = moved[c * TX : (c + 1) * TX]

    each_peer(lambda k: cur_copy(k).wait_recv())
    mean = jnp.sum(got[...].astype(F32), axis=0) * (1.0 / NT)
    tmpl_ref[...] = mean
    windows(1, mean)

    for ds in (-1, 1):
        pl.when(from_side[ds])(rim(ds).wait_recv)
    for j in range(8):
        rows16 = raw[:, 16 * (j // 2) : 16 * (j // 2) + 16].astype(F32)
        eight = rows16[:, 8 * (j % 2) : 8 * (j % 2) + 8].reshape(NT * 8, COLS)
        turned[j] = eight.T.astype(BF16)

    lane = lax.broadcasted_iota(I32, (2 * PL, 128), 1)
    place = lane & 63
    low_half = lane < 64
    step_of = lane & 7
    owner = lax.broadcasted_iota(I32, (NT, 128), 1) >> 3
    pick = (owner == lax.broadcasted_iota(I32, (NT, 128), 0)).astype(F32)

    def correlate(i):
        blocks = []
        for half in range(6):
            x = win[i, half // 2, :, 128 * (half % 2) : 128 * (half % 2) + 128].astype(F32)
            blocks.append(
                jnp.concatenate([pltpu.roll(x, 3, 0), pltpu.roll(x, PL - 5, 0)], axis=0)
            )

        for j3 in range(8):
            lag = j3 - 4
            turn = [pltpu.roll(x, lag % 128, 1) if lag else x for x in blocks]
            other = [pltpu.roll(x, (lag + 64) % 128, 1) for x in blocks]
            if lag > 0:
                inside = place >= lag
            else:
                inside = place < PL + lag
            even = [jnp.where(inside, p, q) for p, q in zip(turn, other)]
            swapped = [jnp.where(inside, q, p) for p, q in zip(turn, other)]
            odd = [
                jnp.where(low_half, swapped[h], swapped[h + 1]).astype(BF16) for h in range(5)
            ]
            even = [x.astype(BF16) for x in even]
            total = jnp.zeros((128, 128), F32)
            for j in range(8):
                rows = slice((j % 2) * PL + 16 * (j // 2), (j % 2) * PL + 16 * (j // 2) + 16)
                stack = []
                for j2 in range(8):
                    off = 8 - j2
                    which = odd if off % 2 else even
                    h = off // 2
                    stack.append(jnp.concatenate([which[h][rows], which[h + 1][rows]], axis=1))
                total += jnp.dot(
                    jnp.concatenate(stack, axis=0), turned[j], preferred_element_type=F32
                )
            for bit in (1, 2, 4):
                total = jnp.where((step_of & bit) != 0, pltpu.roll(total, 128 - bit, 0), total)
            lagged[j3 * 64 : (j3 + 1) * 64] = total.reshape(8, 16, 128)[:, 0:8].reshape(64, 128)
        ordered = jnp.concatenate(
            [
                lagged[pl.ds(j2 * 8 + 7 - j1, 8, stride=64), :]
                for j1 in range(8)
                for j2 in range(8)
            ],
            axis=0,
        )
        sums = lax.dot_general(
            pick, ordered, (((1,), (1,)), ((), ())),
            precision=lax.Precision.HIGHEST, preferred_element_type=F32,
        ) * (1.0 / float(PL) ** 3)
        for k in range(4):
            part[:, 4 * i + k, :] = sums[:, 128 * k : 128 * k + 128]

    for i in range(2):
        for side in range(8):
            win_copy(i, side, "wait_recv")
        correlate(i)

    def part_copy(k):
        to = across_tm(k)
        return remote(part.at[to], gath.at[t], part_send.at[k], part_recv.at[k], (to, s))

    each_peer(lambda k: part_copy(k).start())
    gath[t] = part[t]
    for ds in (-1, 1):
        pl.when(there[ds])(halo(ds).wait_send)
        pl.when(there[ds])(rim(ds).wait_send)
    each_peer(lambda k: raw_copy(k).wait_send())
    each_peer(lambda k: cur_copy(k).wait_send())
    for i in range(2):
        for side in range(8):
            win_copy(i, side, "wait_send")
    each_peer(lambda k: part_copy(k).wait_recv())
    final = jnp.sum(gath[...], axis=0)
    for i in range(2):
        for k in range(4):
            corr_ref[i, 0, :, 128 * k : 128 * k + 128] = final[4 * i + k : 4 * i + k + 1]
    each_peer(lambda k: part_copy(k).wait_send())


def solution(mesh):
    ns = mesh.shape["space"]

    def on_device(volumes, shifts):
        dma = pltpu.SemaphoreType.DMA
        vmem = pltpu.VMEM
        return pl.pallas_call(
            functools.partial(kernel, ns),
            out_shape=(
                jax.ShapeDtypeStruct((2, 1, 1, 512), F32),
                jax.ShapeDtypeStruct((1, TX, PL * PL), BF16),
                jax.ShapeDtypeStruct((TX, COLS), F32),
            ),
            in_specs=[
                pl.BlockSpec(memory_space=pl.ANY),
                pl.BlockSpec(memory_space=pltpu.SMEM),
            ],
            out_specs=(
                pl.BlockSpec(memory_space=pltpu.VMEM),
                pl.BlockSpec(memory_space=pltpu.VMEM),
                pl.BlockSpec(memory_space=pltpu.VMEM),
            ),
            scratch_shapes=[
                vmem((PL, PL * PL), BF16),
                vmem((NT, PL, COLS), BF16),
                vmem((2, TX, PL), BF16),
                vmem((2, 4, COLS, COLS), BF16),
                vmem(((NT + 3) * TX, COLS), BF16),
                vmem((NT, TX, COLS), BF16),
                vmem((NT, TX, COLS), BF16),
                vmem((2, 3, PL, COLS), BF16),
                vmem((8, COLS, 128), BF16),
                vmem((8, 128), F32),
                vmem((512, 128), F32),
                vmem((NT, 8, 128), F32),
                vmem((NT, 8, 128), F32),
                dma,
                dma((2,)), dma((2,)),
                dma((NT,)), dma((NT,)),
                dma((2,)), dma((2,)),
                dma((NT,)), dma((NT,)),
                dma((2, 8)), dma((2, 8)),
                dma((NT,)), dma((NT,)),
            ],
            compiler_params=pltpu.CompilerParams(
                collective_id=0, has_side_effects=True, vmem_limit_bytes=40 * 1024 * 1024
            ),
        )(volumes, shifts)

    return jax.shard_map(
        on_device,
        mesh=mesh,
        in_specs=(P("tm", "space", None), P(None, None, "tm", "space")),
        out_specs=(P(None, "tm", "space", None), P("tm", "space", None), P("space", "tm")),
        check_vma=False,
    )
```

time: 340 us -> 46.6 us (0.14)
  waiting for transfers between devices: 141 us -> 0 us
  local copies, waits for them, and re-layouts: 100 us -> 3.63 us
  starting transfers between devices: 43.2 us -> 0 us
  Pallas kernels: 0 us -> 42.1 us
  between operations: 34 us -> 0.64 us
  matrix products: 12.6 us -> 0 us
  other arithmetic: 7.92 us -> 0 us
    psum x1 -> x0, waiting for transfers between devices: 141 us -> none  [on_device(): lax.psum(partial_value.astype(jnp.bfloat16), 'tm').astype(jnp.float32)]
    reshape x36 -> x0, local copies, waits for them, and re-layouts: 88.6 us -> none  [the longest x24 67.2 us: rotate_axes(): array.reshape(stacked, leading, middle, trailing).transpose(0, 2, 3, 1)]
    ppermute x6 -> x0, starting transfers between devices: 43 us -> none  [the longest x3 37 us: extended(): lax.ppermute(tail, axis, [(i, (i + 1) % count) for i in range(ends)])]
    pallas_call x0 -> x1, Pallas kernels: none -> 42.1 us  [on_device(): pl.pallas_call(functools.partial(kernel, ns), out_shape=(jax.ShapeDtypeSt...]
    dot_general x19 -> x0, matrix products: 12.6 us -> none  [the longest x3 3.27 us: later_sections(): jnp.dot(t_next, third, preferred_element_type=jnp.float32)]
    another operation x4 -> x0, other arithmetic: 4.98 us -> none
    unnamed x6, local copies, waits for them, and re-layouts: 0.01 us -> 3.63 us
  transfers between devices with their start and end apart: 7 -> 0, of which waited for: 1 -> 0; matrix products, arithmetic and copies ran while one was open for 16% -> 0% of each run, Pallas kernels for 0% -> 0%
where the time goes in v1:
time: 46.6 us; the launch traced here: 46.4 us
  Pallas kernels  42.1 us (90%)
  local copies, waits for them, and re-layouts  3.63 us (8%)
  between operations  0.64 us (1%)
    pallas_call x1, Pallas kernels, on_device(): pl.pallas_call(functools.partial(kernel, ns), out_shape=(jax.ShapeDtypeSt...  42.1 us
    unnamed x6, local copies, waits for them, and re-layouts  3.63 us

profile of v1, /device:TPU:57, one launch (start us, length us, event | category | flops | bytes accessed | tf_op | source)
XLA Modules:
  0.0 46.4 jit_solution(17893164342342563745)
XLA Ops:
  0.6 0.8 %copy.5.shift_ref = s32[2,3,1,1]{3,2,1,0:T(1,128)S(1)} copy(s32[2,3,1,1]{1,3,2,0:T(1,128)} %param.3) | data formatting | bytes 48 | tf_op args[1]
  1.4 0.0 copy-start
  1.4 0.9 %copy-done = bf16[1,32,4096]{2,1,0:T(8,128)(2,1)S(1)} copy-done((bf16[1,32,4096]{2,1,0:T(8,128)(2,1)S(1)}, bf16[1,32,4096]{2,1,0:T(8,128)(2,1)}, u32[]{:S(2)}) %copy-start) | copy-done | bytes 262168
  2.4 42.1 %shard_map.49 = (f32[2,1,1,512]{3,2,1,0:T(1,128)S(1)}, bf16[1,32,4096]{2,1,0:T(8,128)(2,1)S(1)}, f32[32,256]{1,0:T(8,128)S(1)}) custom-call(bf16[1,32,4096]{2,1,0:T(8,128)(2,1)S(1)} %copy-done, s32[2,3,1,1]{3,2,1,0:T(1,128)S(1)} %copy.5.shift_ref), custom_call_target="tpu_custom_call" | custom-call | tf_op jit(solution)/shard_map/pallas_call | solution.py:286
  44.5 0.6 %copy.9 = f32[2,1,1,512]{3,2,1,0:T(1,128)} copy(f32[2,1,1,512]{3,2,1,0:T(1,128)S(1)} %get-tuple-element.6) | data formatting | bytes 8192
  45.1 0.7 %copy.10 = bf16[1,32,4096]{2,1,0:T(8,128)(2,1)} copy(bf16[1,32,4096]{2,1,0:T(8,128)(2,1)S(1)} %get-tuple-element.7) | data formatting | bytes 524288
  45.8 0.6 %copy.11 = f32[32,256]{1,0:T(8,128)} copy(f32[32,256]{1,0:T(8,128)S(1)} %get-tuple-element.8) | data formatting | bytes 65536
Async XLA Ops:
  1.4 0.9 %copy-start = (bf16[1,32,4096]{2,1,0:T(8,128)(2,1)S(1)}, bf16[1,32,4096]{2,1,0:T(8,128)(2,1)}, u32[]{:S(2)}) copy-start(bf16[1,32,4096]{2,1,0:T(8,128)(2,1)} %vol_ref.1) | copy-start | bytes 786436

commit v2 on v1

--- a/solution.py
+++ b/solution.py
@@ -15,6 +15,12 @@
 HALO = 16
 NT = 16
 COLS = 256
+EDGE = 8
+HALF = PL * PL // 2
+OFFSETS = (
+    (2, 2), (2, 1), (2, 3), (1, 2), (3, 2), (1, 1), (1, 3), (3, 1), (3, 3),
+    (0, 2), (0, 1), (0, 3), (2, 0), (1, 0), (3, 0),
+)
 SIDES = tuple((dt, ds) for ds in (-1, 1, 0) for dt in (-1, 0, 1) if (dt, ds) != (0, 0))
 
 
@@ -26,27 +32,38 @@
     )
 
 
+def snake(t):
+    z = lax.rem(t, 4)
+    return t + lax.rem(t // 4, 2) * (3 - 2 * z)
+
+
 def kernel(
     ns, vol_ref, shift_ref, corr_ref, reg_ref, tmpl_ref,
-    patch, raw, across, planes, xw, cur, got, win, turned, rolled, lagged, part, gath,
-    local_sem, halo_send, halo_recv, raw_send, raw_recv, rim_send, rim_recv,
-    cur_send, cur_recv, win_send, win_recv, part_send, part_recv,
+    patch, edge_out, edge, raw, across, planes, xw, cur, got, win, turned, mean_out,
+    moved, lagged, part, gath,
+    local_sem, moved_sem, halo_send, halo_recv, raw_send, raw_recv, rim_send, rim_recv,
+    cur_send, cur_recv, win_send, win_recv, mean_send, mean_recv, part_send, part_recv,
 ):
     t = lax.axis_index("tm")
     s = lax.axis_index("space")
+    chunk = snake(t)
     has_lo, has_hi = s > 0, s < ns - 1
     there = {-1: has_lo, 1: has_hi}
     from_side = {-1: has_hi, 1: has_lo}
 
-    def across_tm(k):
-        return lax.rem(t + k + NT, NT)
+    def peer(k):
+        dx, dz = OFFSETS[k]
+        return 4 * lax.rem(t // 4 + dx, 4) + lax.rem(lax.rem(t, 4) + dz, 4)
+
+    def beside(dt):
+        return snake(lax.rem(chunk + dt + NT, NT))
+
+    def columns(to):
+        return pl.ds(pl.multiple_of(snake(to) * COLS, COLS), COLS)
 
     def each_peer(body):
-        def step(k, carry):
+        for k in range(NT - 1):
             body(k)
-            return carry
-
-        lax.fori_loop(1, NT, step, 0)
 
     def remote(src, dst, send, recv, peer):
         return pltpu.make_async_remote_copy(
@@ -54,13 +71,13 @@
             device_id=peer, device_id_type=MESH,
         )
 
-    own = pltpu.make_async_copy(vol_ref.at[0], patch.at[pl.ds(HALO, TX)], local_sem)
+    own = pltpu.make_async_copy(vol_ref.at[0], patch, local_sem)
     own.start()
 
     barrier = pltpu.get_barrier_semaphore()
     each_peer(
         lambda k: pl.semaphore_signal(
-            barrier, inc=1, device_id=(across_tm(k), s), device_id_type=MESH
+            barrier, inc=1, device_id=(peer(k), s), device_id_type=MESH
         )
     )
     for ds in (-1, 1):
@@ -69,61 +86,68 @@
         def _():
             for dt in (-1, 0, 1):
                 pl.semaphore_signal(
-                    barrier, inc=1, device_id=(across_tm(dt), s + ds), device_id_type=MESH
+                    barrier, inc=1, device_id=(beside(dt), s + ds), device_id_type=MESH
                 )
 
     row = lax.broadcasted_iota(I32, (TX, PL), 0)
     col = lax.broadcasted_iota(I32, (TX, PL), 1)
+    which = (col & 15) >> 3
+    margin = jnp.where(col < 48, -EDGE, TX) + (col & 7)
+    source = [
+        jnp.where(col < TX, col, jnp.where(which == half, margin, 2 * PL)) for half in range(2)
+    ]
     a = lax.broadcasted_iota(I32, (COLS, COLS), 0)
     b = lax.broadcasted_iota(I32, (COLS, COLS), 1)
     for i in range(2):
-        across[i] = band(shift_ref[i, 0, 0, 0], row + HALO - col).astype(BF16)
-        third = band(shift_ref[i, 2, 0, 0], (b & 63) - (a & 63))
+        for half in range(2):
+            across[i, half] = band(shift_ref[i, 0, 0, 0], row - source[half]).astype(BF16)
+        third = band(shift_ref[i, 0, 0, 2], (b & 63) - (a & 63))
         for d in range(4):
-            second = band(shift_ref[i, 1, 0, 0], (b >> 6) - (a >> 6) - 4 * (d - 2))
+            second = band(shift_ref[i, 0, 0, 1], (b >> 6) - (a >> 6) - 4 * (d - 2))
             planes[i, d] = (second * third).astype(BF16)
     xw[0:64] = jnp.zeros((64, COLS), BF16)
     xw[18 * TX : 19 * TX] = jnp.zeros((TX, COLS), BF16)
-    for ds, at in ((-1, 0), (1, 48)):
+    for k, ds, at in ((0, -1, 0), (1, 1, 48)):
 
         @pl.when(jnp.logical_not(there[ds]))
         def _():
-            patch[at : at + HALO] = jnp.zeros((HALO, PL * PL), BF16)
+            edge[k] = jnp.zeros((HALO, HALF), BF16)
             raw[:, at : at + HALO] = jnp.zeros((NT, HALO, COLS), BF16)
             win[:, :, at : at + HALO] = jnp.zeros((2, 3, HALO, COLS), BF16)
 
     own.wait()
+    for k in range(2):
+        wide = patch[HALO * k : HALO * k + HALO].astype(F32)[EDGE * k : EDGE * k + EDGE]
+        edge_out[k] = jnp.concatenate([wide[:, :HALF], wide[:, HALF:]], axis=0).astype(BF16)
     pl.semaphore_wait(barrier, NT - 1 + 3 * (has_lo.astype(I32) + has_hi.astype(I32)))
 
     def halo(ds):
-        src, dst = (HALO, 48) if ds < 0 else (TX, 0)
         k = 0 if ds < 0 else 1
         return remote(
-            patch.at[pl.ds(src, HALO)], patch.at[pl.ds(dst, HALO)],
-            halo_send.at[k], halo_recv.at[k], (t, s + ds),
+            edge_out.at[k], edge.at[1 - k], halo_send.at[k], halo_recv.at[k], (t, s + ds)
         )
 
     def raw_copy(k):
-        to = across_tm(k)
+        to = peer(k)
         return remote(
-            patch.at[pl.ds(HALO, TX), pl.ds(pl.multiple_of(to * COLS, COLS), COLS)],
-            raw.at[t, pl.ds(HALO, TX)],
+            patch.at[:, columns(to)], raw.at[t, pl.ds(HALO, TX)],
             raw_send.at[k], raw_recv.at[k], (to, s),
         )
 
     for ds in (-1, 1):
         pl.when(there[ds])(halo(ds).start)
     each_peer(lambda k: raw_copy(k).start())
-    raw[t, HALO : HALO + TX] = patch[
-        HALO : HALO + TX, pl.ds(pl.multiple_of(t * COLS, COLS), COLS)
-    ]
+    raw[t, HALO : HALO + TX] = patch[:, columns(t)]
     for ds in (-1, 1):
         pl.when(from_side[ds])(halo(ds).wait_recv)
 
     def warp(i):
         for c in range(NT):
+            half, at = c // 8, (c % 8) * COLS
+            rows = [patch[:, c * COLS : (c + 1) * COLS]]
+            rows += [edge[k, :, at : at + COLS] for k in range(2)]
             xw[(c + 2) * TX : (c + 3) * TX] = jnp.dot(
-                across[i], patch[:, c * COLS : (c + 1) * COLS], preferred_element_type=F32
+                across[i, half], jnp.concatenate(rows, axis=0), preferred_element_type=F32
             ).astype(BF16)
         total = jnp.dot(xw[0 : NT * TX], planes[i, 0], preferred_element_type=F32)
         for d in range(1, 4):
@@ -135,11 +159,11 @@
     cur[...] = warp(0).reshape(NT, TX, COLS)
 
     def cur_copy(k):
-        to = across_tm(k)
-        return remote(cur.at[to], got.at[t], cur_send.at[k], cur_recv.at[k], (to, s))
+        to = peer(k)
+        return remote(cur.at[snake(to)], got.at[t], cur_send.at[k], cur_recv.at[k], (to, s))
 
     each_peer(lambda k: cur_copy(k).start())
-    got[t] = cur[t]
+    got[t] = cur[chunk]
 
     def win_copy(i, side, act):
         dt, ds = SIDES[side]
@@ -148,7 +172,7 @@
         rows = TX if ds == 0 else HALO
         copy = remote(
             win.at[i, 1, pl.ds(src, rows)], win.at[i, 1 - dt, pl.ds(dst, rows)],
-            win_send.at[i, side], win_recv.at[i, side], (across_tm(dt), s + ds),
+            win_send.at[i, side], win_recv.at[i, side], (beside(dt), s + ds),
         )
         present = (from_side if act == "wait_recv" else there).get(ds)
         if present is None:
@@ -175,14 +199,23 @@
     for ds in (-1, 1):
         pl.when(there[ds])(rim(ds).start)
 
-    moved = warp(1)
+    second_warp = warp(1)
     for c in range(NT):
-        reg_ref[0, :, c * COLS : (c + 1) * COLS] = moved[c * TX : (c + 1) * TX]
+        moved[0, :, c * COLS : (c + 1) * COLS] = second_warp[c * TX : (c + 1) * TX]
+    put_moved = pltpu.make_async_copy(moved, reg_ref, moved_sem)
+    put_moved.start()
 
     each_peer(lambda k: cur_copy(k).wait_recv())
     mean = jnp.sum(got[...].astype(F32), axis=0) * (1.0 / NT)
-    tmpl_ref[...] = mean
     windows(1, mean)
+    to_place = remote(
+        mean_out, tmpl_ref, mean_send, mean_recv, (chunk, s)
+    )
+
+    put_mean = pltpu.make_async_copy(mean_out, tmpl_ref, local_sem)
+    mean_out[...] = mean
+    pl.when(chunk == t)(put_mean.start)
+    pl.when(chunk != t)(to_place.start)
 
     for ds in (-1, 1):
         pl.when(from_side[ds])(rim(ds).wait_recv)
@@ -191,10 +224,10 @@
         eight = rows16[:, 8 * (j % 2) : 8 * (j % 2) + 8].reshape(NT * 8, COLS)
         turned[j] = eight.T.astype(BF16)
 
-    lane = lax.broadcasted_iota(I32, (2 * PL, 128), 1)
+    lane = lax.broadcasted_iota(I32, (PL, 128), 1)
     place = lane & 63
     low_half = lane < 64
-    step_of = lane & 7
+    step_of = lax.broadcasted_iota(I32, (128, 128), 1) & 7
     owner = lax.broadcasted_iota(I32, (NT, 128), 1) >> 3
     pick = (owner == lax.broadcasted_iota(I32, (NT, 128), 0)).astype(F32)
 
@@ -202,9 +235,10 @@
         blocks = []
         for half in range(6):
             x = win[i, half // 2, :, 128 * (half % 2) : 128 * (half % 2) + 128].astype(F32)
-            blocks.append(
-                jnp.concatenate([pltpu.roll(x, 3, 0), pltpu.roll(x, PL - 5, 0)], axis=0)
-            )
+            blocks.append(pltpu.roll(x, 3, 0))
+
+        def both(x):
+            return jnp.concatenate([x, x[8:], x[:8]], axis=0).astype(BF16)
 
         for j3 in range(8):
             lag = j3 - 4
@@ -217,9 +251,9 @@
             even = [jnp.where(inside, p, q) for p, q in zip(turn, other)]
             swapped = [jnp.where(inside, q, p) for p, q in zip(turn, other)]
             odd = [
-                jnp.where(low_half, swapped[h], swapped[h + 1]).astype(BF16) for h in range(5)
+                both(jnp.where(low_half, swapped[h], swapped[h + 1])) for h in range(5)
             ]
-            even = [x.astype(BF16) for x in even]
+            even = [x if h == 0 else both(x) for h, x in enumerate(even)]
             total = jnp.zeros((128, 128), F32)
             for j in range(8):
                 rows = slice((j % 2) * PL + 16 * (j // 2), (j % 2) * PL + 16 * (j // 2) + 16)
@@ -256,7 +290,7 @@
         correlate(i)
 
     def part_copy(k):
-        to = across_tm(k)
+        to = peer(k)
         return remote(part.at[to], gath.at[t], part_send.at[k], part_recv.at[k], (to, s))
 
     each_peer(lambda k: part_copy(k).start())
@@ -275,6 +309,18 @@
         for k in range(4):
             corr_ref[i, 0, :, 128 * k : 128 * k + 128] = final[4 * i + k : 4 * i + k + 1]
     each_peer(lambda k: part_copy(k).wait_send())
+    pl.when(chunk == t)(put_mean.wait)
+    pl.when(chunk != t)(to_place.wait)
+    put_moved.wait()
+
+
+def put(*refs):
+    *arrays, sems = refs
+    copies = [pltpu.make_async_copy(arrays[k], arrays[k + 3], sems.at[k]) for k in range(3)]
+    for copy in copies:
+        copy.start()
+    for copy in copies:
+        copy.wait()
 
 
 def solution(mesh):
@@ -283,7 +329,7 @@
     def on_device(volumes, shifts):
         dma = pltpu.SemaphoreType.DMA
         vmem = pltpu.VMEM
-        return pl.pallas_call(
+        results = pl.pallas_call(
             functools.partial(kernel, ns),
             out_shape=(
                 jax.ShapeDtypeStruct((2, 1, 1, 512), F32),
@@ -296,35 +342,46 @@
             ],
             out_specs=(
                 pl.BlockSpec(memory_space=pltpu.VMEM),
-                pl.BlockSpec(memory_space=pltpu.VMEM),
-                pl.BlockSpec(memory_space=pltpu.VMEM),
+                pl.BlockSpec(memory_space=pl.ANY),
+                pl.BlockSpec(memory_space=pl.ANY),
             ),
             scratch_shapes=[
-                vmem((PL, PL * PL), BF16),
+                vmem((TX, PL * PL), BF16),
+                vmem((2, HALO, HALF), BF16),
+                vmem((2, HALO, HALF), BF16),
                 vmem((NT, PL, COLS), BF16),
-                vmem((2, TX, PL), BF16),
+                vmem((2, 2, TX, PL), BF16),
                 vmem((2, 4, COLS, COLS), BF16),
                 vmem(((NT + 3) * TX, COLS), BF16),
                 vmem((NT, TX, COLS), BF16),
                 vmem((NT, TX, COLS), BF16),
                 vmem((2, 3, PL, COLS), BF16),
                 vmem((8, COLS, 128), BF16),
-                vmem((8, 128), F32),
+                vmem((TX, COLS), F32),
+                vmem((1, TX, PL * PL), BF16),
                 vmem((512, 128), F32),
                 vmem((NT, 8, 128), F32),
                 vmem((NT, 8, 128), F32),
-                dma,
+                dma, dma,
                 dma((2,)), dma((2,)),
                 dma((NT,)), dma((NT,)),
                 dma((2,)), dma((2,)),
                 dma((NT,)), dma((NT,)),
                 dma((2, 8)), dma((2, 8)),
+                dma, dma,
                 dma((NT,)), dma((NT,)),
             ],
             compiler_params=pltpu.CompilerParams(
-                collective_id=0, has_side_effects=True, vmem_limit_bytes=40 * 1024 * 1024
+                collective_id=0, has_side_effects=True, vmem_limit_bytes=63 * 1024 * 1024
             ),
-        )(volumes, shifts)
+        )(volumes, shifts.transpose(0, 2, 3, 1))
+        return pl.pallas_call(
+            put,
+            out_shape=tuple(jax.ShapeDtypeStruct(x.shape, x.dtype) for x in results),
+            in_specs=[pl.BlockSpec(memory_space=pl.ANY)] * 3,
+            out_specs=(pl.BlockSpec(memory_space=pl.ANY),) * 3,
+            scratch_shapes=[dma((3,))],
+        )(*results)
 
     return jax.shard_map(
         on_device,

time: 46.6 us -> 50.5 us (1.084)
  Pallas kernels: 42.1 us -> 49.7 us
  local copies, waits for them, and re-layouts: 3.63 us -> 0 us
    pallas_call x0 -> x1, Pallas kernels: none -> 10.2 us  [on_device(): pl.pallas_call(put, out_shape=tuple((jax.ShapeDtypeStruct(x.shape, x.dtyp...]
    unnamed x6 -> x0, local copies, waits for them, and re-layouts: 3.63 us -> none
    pallas_call x1, Pallas kernels: 42.1 us -> 39.5 us  [on_device(): pl.pallas_call(functools.partial(kernel, ns), out_shape=(jax.ShapeDtypeSt...]
where the time goes in v2:
time: 50.5 us; the launch traced here: 50.3 us
  Pallas kernels  49.7 us (98%)
  between operations  0.64 us (1%)
    pallas_call x1, Pallas kernels, on_device(): pl.pallas_call(functools.partial(kernel, ns), out_shape=(jax.ShapeDtypeSt...  39.5 us
    pallas_call x1, Pallas kernels, on_device(): pl.pallas_call(put, out_shape=tuple((jax.ShapeDtypeStruct(x.shape, x.dtyp...  10.2 us

profile of v2, /device:TPU:57, one launch (start us, length us, event | category | flops | bytes accessed | tf_op | source)
XLA Modules:
  0.0 50.3 jit_solution(14774014327418157554)
XLA Ops:
  0.6 39.5 %shard_map.49 = (f32[2,1,1,512]{3,2,1,0:T(1,128)}, bf16[1,32,4096]{2,1,0:T(8,128)(2,1)}, f32[32,256]{1,0:T(8,128)}) custom-call(bf16[1,32,4096]{2,1,0:T(8,128)(2,1)} %vol_ref.1, s32[2,1,1,3]{3,2,1,0:T(1,128)} %bitcast.3), custom_call_target="tpu_custom_call" | custom-call | tf_op jit(solution)/shard_map/pallas_call | solution.py:332
  40.1 10.2 %shard_map.50 = (f32[2,1,1,512]{3,2,1,0:T(1,128)}, bf16[1,32,4096]{2,1,0:T(8,128)(2,1)}, f32[32,256]{1,0:T(8,128)}) custom-call(f32[2,1,1,512]{3,2,1,0:T(1,128)} %get-tuple-element.6.refs_0_, bf16[1,32,4096]{2,1,0:T(8,128)(2,1)} %get-tuple-element.7.refs_1_, f32[32,256]{1,0:T(8,128)} %get-tuple-element.8.refs_2_), custom_call_target="tpu_custom_call" | custom-call | tf_op jit(solution)/shard_map/pallas_call | solution.py:378

commit v3 on v2

--- a/solution.py
+++ b/solution.py
@@ -372,7 +372,7 @@
                 dma((NT,)), dma((NT,)),
             ],
             compiler_params=pltpu.CompilerParams(
-                collective_id=0, has_side_effects=True, vmem_limit_bytes=63 * 1024 * 1024
+                collective_id=0, has_side_effects=True, vmem_limit_bytes=40 * 1024 * 1024
             ),
         )(volumes, shifts.transpose(0, 2, 3, 1))
         return pl.pallas_call(
@@ -381,6 +381,7 @@
             in_specs=[pl.BlockSpec(memory_space=pl.ANY)] * 3,
             out_specs=(pl.BlockSpec(memory_space=pl.ANY),) * 3,
             scratch_shapes=[dma((3,))],
+            compiler_params=pltpu.CompilerParams(vmem_limit_bytes=1024 * 1024),
         )(*results)
 
     return jax.shard_map(

time: 50.5 us -> 41.9 us (0.83)
  Pallas kernels: 49.7 us -> 39.5 us
  local copies, waits for them, and re-layouts: 0 us -> 1.62 us
    pallas_call x1, Pallas kernels: 10.2 us -> 0.74 us  [on_device(): pl.pallas_call(put, out_shape=tuple((jax.ShapeDtypeStruct(x.shape, x.dtyp...]
    unnamed x0 -> x4, local copies, waits for them, and re-layouts: none -> 1.62 us
    pallas_call x1, Pallas kernels: 39.5 us -> 38.8 us  [on_device(): pl.pallas_call(functools.partial(kernel, ns), out_shape=(jax.ShapeDtypeSt...]
where the time goes in v3:
time: 41.9 us; the launch traced here: 41.8 us
  Pallas kernels  39.5 us (94%)
  local copies, waits for them, and re-layouts  1.62 us (4%)
  between operations  0.65 us (2%)
    pallas_call x1, Pallas kernels, on_device(): pl.pallas_call(functools.partial(kernel, ns), out_shape=(jax.ShapeDtypeSt...  38.8 us
    unnamed x4, local copies, waits for them, and re-layouts  1.62 us

profile of v3, /device:TPU:57, one launch (start us, length us, event | category | flops | bytes accessed | tf_op | source)
XLA Modules:
  0.0 41.8 jit_solution(10908707995607858394)
XLA Ops:
  0.6 0.0 copy-start.1
  0.6 0.7 %copy-done.1 = s32[2,3,1,1]{1,3,2,0:T(1,128)S(1)} copy-done((s32[2,3,1,1]{1,3,2,0:T(1,128)S(1)}, s32[2,3,1,1]{1,3,2,0:T(1,128)}, u32[]{:S(2)}) %copy-start.1) | copy-done | bytes 48
  1.3 0.0 copy-start
  1.3 0.9 %copy-done = bf16[1,32,4096]{2,1,0:T(8,128)(2,1)S(1)} copy-done((bf16[1,32,4096]{2,1,0:T(8,128)(2,1)S(1)}, bf16[1,32,4096]{2,1,0:T(8,128)(2,1)}, u32[]{:S(2)}) %copy-start) | copy-done | bytes 262168
  2.3 38.8 %shard_map.49 = (f32[2,1,1,512]{3,2,1,0:T(1,128)S(1)}, bf16[1,32,4096]{2,1,0:T(8,128)(2,1)S(1)}, f32[32,256]{1,0:T(8,128)S(1)}) custom-call(bf16[1,32,4096]{2,1,0:T(8,128)(2,1)S(1)} %copy-done, s32[2,1,1,3]{3,2,1,0:T(1,128)S(1)} %bitcast.3), custom_call_target="tpu_custom_call" | custom-call | tf_op jit(solution)/shard_map/pallas_call | solution.py:332
  41.0 0.7 %shard_map.50 = (f32[2,1,1,512]{3,2,1,0:T(1,128)}, bf16[1,32,4096]{2,1,0:T(8,128)(2,1)}, f32[32,256]{1,0:T(8,128)}) custom-call(f32[2,1,1,512]{3,2,1,0:T(1,128)S(1)} %get-tuple-element.6.refs_0_, bf16[1,32,4096]{2,1,0:T(8,128)(2,1)S(1)} %get-tuple-element.7.refs_1_, f32[32,256]{1,0:T(8,128)S(1)} %get-tuple-element.8.refs_2_), custom_call_target="tpu_custom_call" | custom-call | tf_op jit(solution)/shard_map/pallas_call | solution.py:378
Async XLA Ops:
  0.6 0.7 %copy-start.1 = (s32[2,3,1,1]{1,3,2,0:T(1,128)S(1)}, s32[2,3,1,1]{1,3,2,0:T(1,128)}, u32[]{:S(2)}) copy-start(s32[2,3,1,1]{1,3,2,0:T(1,128)} %param.3) | copy-start | bytes 76
  1.3 0.9 %copy-start = (bf16[1,32,4096]{2,1,0:T(8,128)(2,1)S(1)}, bf16[1,32,4096]{2,1,0:T(8,128)(2,1)}, u32[]{:S(2)}) copy-start(bf16[1,32,4096]{2,1,0:T(8,128)(2,1)} %vol_ref.1) | copy-start | bytes 786436

commit v4 on v3

--- a/solution.py
+++ b/solution.py
@@ -39,9 +39,9 @@
 
 def kernel(
     ns, vol_ref, shift_ref, corr_ref, reg_ref, tmpl_ref,
-    patch, edge_out, edge, raw, across, planes, xw, cur, got, win, turned, mean_out,
-    moved, lagged, part, gath,
-    local_sem, moved_sem, halo_send, halo_recv, raw_send, raw_recv, rim_send, rim_recv,
+    edge_out, edge, raw, across, planes, xw, cur, got, win, turned, mean_out,
+    lagged, part, gath,
+    local_sem, halo_send, halo_recv, raw_send, raw_recv, rim_send, rim_recv,
     cur_send, cur_recv, win_send, win_recv, mean_send, mean_recv, part_send, part_recv,
 ):
     t = lax.axis_index("tm")
@@ -71,9 +71,6 @@
             device_id=peer, device_id_type=MESH,
         )
 
-    own = pltpu.make_async_copy(vol_ref.at[0], patch, local_sem)
-    own.start()
-
     barrier = pltpu.get_barrier_semaphore()
     each_peer(
         lambda k: pl.semaphore_signal(
@@ -88,6 +85,29 @@
                 pl.semaphore_signal(
                     barrier, inc=1, device_id=(beside(dt), s + ds), device_id_type=MESH
                 )
+
+    for k in range(2):
+        wide = vol_ref[0, HALO * k : HALO * k + HALO].astype(F32)[EDGE * k : EDGE * k + EDGE]
+        edge_out[k] = jnp.concatenate([wide[:, :HALF], wide[:, HALF:]], axis=0).astype(BF16)
+    pl.semaphore_wait(barrier, NT - 1 + 3 * (has_lo.astype(I32) + has_hi.astype(I32)))
+
+    def halo(ds):
+        k = 0 if ds < 0 else 1
+        return remote(
+            edge_out.at[k], edge.at[1 - k], halo_send.at[k], halo_recv.at[k], (t, s + ds)
+        )
+
+    def raw_copy(k):
+        to = peer(k)
+        return remote(
+            vol_ref.at[0, :, columns(to)], raw.at[t, pl.ds(HALO, TX)],
+            raw_send.at[k], raw_recv.at[k], (to, s),
+        )
+
+    for ds in (-1, 1):
+        pl.when(there[ds])(halo(ds).start)
+    each_peer(lambda k: raw_copy(k).start())
+    raw[t, HALO : HALO + TX] = vol_ref[0, :, columns(t)]
 
     row = lax.broadcasted_iota(I32, (TX, PL), 0)
     col = lax.broadcasted_iota(I32, (TX, PL), 1)
@@ -114,37 +134,13 @@
             edge[k] = jnp.zeros((HALO, HALF), BF16)
             raw[:, at : at + HALO] = jnp.zeros((NT, HALO, COLS), BF16)
             win[:, :, at : at + HALO] = jnp.zeros((2, 3, HALO, COLS), BF16)
-
-    own.wait()
-    for k in range(2):
-        wide = patch[HALO * k : HALO * k + HALO].astype(F32)[EDGE * k : EDGE * k + EDGE]
-        edge_out[k] = jnp.concatenate([wide[:, :HALF], wide[:, HALF:]], axis=0).astype(BF16)
-    pl.semaphore_wait(barrier, NT - 1 + 3 * (has_lo.astype(I32) + has_hi.astype(I32)))
-
-    def halo(ds):
-        k = 0 if ds < 0 else 1
-        return remote(
-            edge_out.at[k], edge.at[1 - k], halo_send.at[k], halo_recv.at[k], (t, s + ds)
-        )
-
-    def raw_copy(k):
-        to = peer(k)
-        return remote(
-            patch.at[:, columns(to)], raw.at[t, pl.ds(HALO, TX)],
-            raw_send.at[k], raw_recv.at[k], (to, s),
-        )
-
-    for ds in (-1, 1):
-        pl.when(there[ds])(halo(ds).start)
-    each_peer(lambda k: raw_copy(k).start())
-    raw[t, HALO : HALO + TX] = patch[:, columns(t)]
     for ds in (-1, 1):
         pl.when(from_side[ds])(halo(ds).wait_recv)
 
     def warp(i):
         for c in range(NT):
             half, at = c // 8, (c % 8) * COLS
-            rows = [patch[:, c * COLS : (c + 1) * COLS]]
+            rows = [vol_ref[0, :, c * COLS : (c + 1) * COLS]]
             rows += [edge[k, :, at : at + COLS] for k in range(2)]
             xw[(c + 2) * TX : (c + 3) * TX] = jnp.dot(
                 across[i, half], jnp.concatenate(rows, axis=0), preferred_element_type=F32
@@ -201,9 +197,7 @@
 
     second_warp = warp(1)
     for c in range(NT):
-        moved[0, :, c * COLS : (c + 1) * COLS] = second_warp[c * TX : (c + 1) * TX]
-    put_moved = pltpu.make_async_copy(moved, reg_ref, moved_sem)
-    put_moved.start()
+        reg_ref[0, :, c * COLS : (c + 1) * COLS] = second_warp[c * TX : (c + 1) * TX]
 
     each_peer(lambda k: cur_copy(k).wait_recv())
     mean = jnp.sum(got[...].astype(F32), axis=0) * (1.0 / NT)
@@ -212,8 +206,8 @@
         mean_out, tmpl_ref, mean_send, mean_recv, (chunk, s)
     )
 
+    mean_out[...] = mean
     put_mean = pltpu.make_async_copy(mean_out, tmpl_ref, local_sem)
-    mean_out[...] = mean
     pl.when(chunk == t)(put_mean.start)
     pl.when(chunk != t)(to_place.start)
 
@@ -229,7 +223,7 @@
     low_half = lane < 64
     step_of = lax.broadcasted_iota(I32, (128, 128), 1) & 7
     owner = lax.broadcasted_iota(I32, (NT, 128), 1) >> 3
-    pick = (owner == lax.broadcasted_iota(I32, (NT, 128), 0)).astype(F32)
+    pick = (owner == lax.broadcasted_iota(I32, (NT, 128), 0)).astype(BF16)
 
     def correlate(i):
         blocks = []
@@ -277,9 +271,13 @@
             ],
             axis=0,
         )
-        sums = lax.dot_general(
-            pick, ordered, (((1,), (1,)), ((), ())),
-            precision=lax.Precision.HIGHEST, preferred_element_type=F32,
+        upper = ordered.astype(BF16)
+        lower = (ordered - upper.astype(F32)).astype(BF16)
+        sums = sum(
+            lax.dot_general(
+                pick, x, (((1,), (1,)), ((), ())), preferred_element_type=F32
+            )
+            for x in (upper, lower)
         ) * (1.0 / float(PL) ** 3)
         for k in range(4):
             part[:, 4 * i + k, :] = sums[:, 128 * k : 128 * k + 128]
@@ -311,7 +309,6 @@
     each_peer(lambda k: part_copy(k).wait_send())
     pl.when(chunk == t)(put_mean.wait)
     pl.when(chunk != t)(to_place.wait)
-    put_moved.wait()
 
 
 def put(*refs):
@@ -337,16 +334,15 @@
                 jax.ShapeDtypeStruct((TX, COLS), F32),
             ),
             in_specs=[
-                pl.BlockSpec(memory_space=pl.ANY),
+                pl.BlockSpec(memory_space=pltpu.VMEM),
                 pl.BlockSpec(memory_space=pltpu.SMEM),
             ],
             out_specs=(
                 pl.BlockSpec(memory_space=pltpu.VMEM),
-                pl.BlockSpec(memory_space=pl.ANY),
-                pl.BlockSpec(memory_space=pl.ANY),
+                pl.BlockSpec(memory_space=pltpu.VMEM),
+                pl.BlockSpec(memory_space=pltpu.VMEM),
             ),
             scratch_shapes=[
-                vmem((TX, PL * PL), BF16),
                 vmem((2, HALO, HALF), BF16),
                 vmem((2, HALO, HALF), BF16),
                 vmem((NT, PL, COLS), BF16),
@@ -358,11 +354,10 @@
                 vmem((2, 3, PL, COLS), BF16),
                 vmem((8, COLS, 128), BF16),
                 vmem((TX, COLS), F32),
-                vmem((1, TX, PL * PL), BF16),
                 vmem((512, 128), F32),
                 vmem((NT, 8, 128), F32),
                 vmem((NT, 8, 128), F32),
-                dma, dma,
+                dma,
                 dma((2,)), dma((2,)),
                 dma((NT,)), dma((NT,)),
                 dma((2,)), dma((2,)),

time: 41.9 us -> 41.8 us (level)
  no operation moved by 1% of the time
where the time goes in v4:
time: 41.8 us; the launch traced here: 41.6 us
  Pallas kernels  39.3 us (94%)
  local copies, waits for them, and re-layouts  1.62 us (4%)
  between operations  0.65 us (2%)
    pallas_call x1, Pallas kernels, on_device(): pl.pallas_call(functools.partial(kernel, ns), out_shape=(jax.ShapeDtypeSt...  38.6 us
    unnamed x4, local copies, waits for them, and re-layouts  1.62 us

profile of v4, /device:TPU:57, one launch (start us, length us, event | category | flops | bytes accessed | tf_op | source)
XLA Modules:
  0.0 41.6 jit_solution(12824737464925589648)
XLA Ops:
  0.6 0.0 copy-start.1
  0.6 0.7 %copy-done.1 = s32[2,3,1,1]{1,3,2,0:T(1,128)S(1)} copy-done((s32[2,3,1,1]{1,3,2,0:T(1,128)S(1)}, s32[2,3,1,1]{1,3,2,0:T(1,128)}, u32[]{:S(2)}) %copy-start.1) | copy-done | bytes 48
  1.3 0.0 copy-start
  1.3 0.9 %copy-done = bf16[1,32,4096]{2,1,0:T(8,128)(2,1)S(1)} copy-done((bf16[1,32,4096]{2,1,0:T(8,128)(2,1)S(1)}, bf16[1,32,4096]{2,1,0:T(8,128)(2,1)}, u32[]{:S(2)}) %copy-start) | copy-done | bytes 262168
  2.3 38.6 %shard_map.49 = (f32[2,1,1,512]{3,2,1,0:T(1,128)S(1)}, bf16[1,32,4096]{2,1,0:T(8,128)(2,1)S(1)}, f32[32,256]{1,0:T(8,128)S(1)}) custom-call(bf16[1,32,4096]{2,1,0:T(8,128)(2,1)S(1)} %copy-done, s32[2,1,1,3]{3,2,1,0:T(1,128)S(1)} %bitcast.3), custom_call_target="tpu_custom_call" | custom-call | tf_op jit(solution)/shard_map/pallas_call | solution.py:329
  40.9 0.7 %shard_map.50 = (f32[2,1,1,512]{3,2,1,0:T(1,128)}, bf16[1,32,4096]{2,1,0:T(8,128)(2,1)}, f32[32,256]{1,0:T(8,128)}) custom-call(f32[2,1,1,512]{3,2,1,0:T(1,128)S(1)} %get-tuple-element.6.refs_0_, bf16[1,32,4096]{2,1,0:T(8,128)(2,1)S(1)} %get-tuple-element.7.refs_1_, f32[32,256]{1,0:T(8,128)S(1)} %get-tuple-element.8.refs_2_), custom_call_target="tpu_custom_call" | custom-call | tf_op jit(solution)/shard_map/pallas_call | solution.py:373
Async XLA Ops:
  0.6 0.7 %copy-start.1 = (s32[2,3,1,1]{1,3,2,0:T(1,128)S(1)}, s32[2,3,1,1]{1,3,2,0:T(1,128)}, u32[]{:S(2)}) copy-start(s32[2,3,1,1]{1,3,2,0:T(1,128)} %param.3) | copy-start | bytes 76
  1.3 0.9 %copy-start = (bf16[1,32,4096]{2,1,0:T(8,128)(2,1)S(1)}, bf16[1,32,4096]{2,1,0:T(8,128)(2,1)}, u32[]{:S(2)}) copy-start(bf16[1,32,4096]{2,1,0:T(8,128)(2,1)} %vol_ref.1) | copy-start | bytes 786436

commit v5 on v4

--- a/solution.py
+++ b/solution.py
@@ -39,10 +39,10 @@
 
 def kernel(
     ns, vol_ref, shift_ref, corr_ref, reg_ref, tmpl_ref,
-    edge_out, edge, raw, across, planes, xw, cur, got, win, turned, mean_out,
+    edge_out, edge, raw, across, planes, xw, cur, got, sums, shares, win, turned, mean_out,
     lagged, part, gath,
     local_sem, halo_send, halo_recv, raw_send, raw_recv, rim_send, rim_recv,
-    cur_send, cur_recv, win_send, win_recv, mean_send, mean_recv, part_send, part_recv,
+    cur_send, cur_recv, share_send, share_recv, win_send, win_recv, mean_send, mean_recv, part_send, part_recv,
 ):
     t = lax.axis_index("tm")
     s = lax.axis_index("space")
@@ -57,6 +57,8 @@
 
     def beside(dt):
         return snake(lax.rem(chunk + dt + NT, NT))
+
+    x, z = t // 4, lax.rem(t, 4)
 
     def columns(to):
         return pl.ds(pl.multiple_of(snake(to) * COLS, COLS), COLS)
@@ -155,11 +157,28 @@
     cur[...] = warp(0).reshape(NT, TX, COLS)
 
     def cur_copy(k):
-        to = peer(k)
-        return remote(cur.at[snake(to)], got.at[t], cur_send.at[k], cur_recv.at[k], (to, s))
-
-    each_peer(lambda k: cur_copy(k).start())
-    got[t] = cur[chunk]
+        to = lax.rem(x + k, 4)
+        return remote(
+            cur.at[pl.ds(4 * to, 4)], got.at[x], cur_send.at[k], cur_recv.at[k],
+            (4 * to + z, s),
+        )
+
+    for k in (2, 1, 3):
+        cur_copy(k).start()
+    got[x] = cur[pl.ds(4 * x, 4)]
+    for k in (1, 3, 2):
+        cur_copy(k).wait_recv()
+    sums[...] = jnp.sum(got[...].astype(F32), axis=0).astype(BF16)
+
+    def share_copy(k):
+        to = 4 * x + lax.rem(z + k, 4)
+        return remote(
+            sums.at[snake(to) - 4 * x], shares.at[z], share_send.at[k], share_recv.at[k], (to, s)
+        )
+
+    for k in (2, 1, 3):
+        share_copy(k).start()
+    shares[z] = sums[chunk - 4 * x]
 
     def win_copy(i, side, act):
         dt, ds = SIDES[side]
@@ -199,8 +218,9 @@
     for c in range(NT):
         reg_ref[0, :, c * COLS : (c + 1) * COLS] = second_warp[c * TX : (c + 1) * TX]
 
-    each_peer(lambda k: cur_copy(k).wait_recv())
-    mean = jnp.sum(got[...].astype(F32), axis=0) * (1.0 / NT)
+    for k in (1, 3, 2):
+        share_copy(k).wait_recv()
+    mean = jnp.sum(shares[...].astype(F32), axis=0) * (1.0 / NT)
     windows(1, mean)
     to_place = remote(
         mean_out, tmpl_ref, mean_send, mean_recv, (chunk, s)
@@ -297,7 +317,9 @@
         pl.when(there[ds])(halo(ds).wait_send)
         pl.when(there[ds])(rim(ds).wait_send)
     each_peer(lambda k: raw_copy(k).wait_send())
-    each_peer(lambda k: cur_copy(k).wait_send())
+    for k in range(1, 4):
+        cur_copy(k).wait_send()
+        share_copy(k).wait_send()
     for i in range(2):
         for side in range(8):
             win_copy(i, side, "wait_send")
@@ -350,7 +372,9 @@
                 vmem((2, 4, COLS, COLS), BF16),
                 vmem(((NT + 3) * TX, COLS), BF16),
                 vmem((NT, TX, COLS), BF16),
-                vmem((NT, TX, COLS), BF16),
+                vmem((4, 4, TX, COLS), BF16),
+                vmem((4, TX, COLS), BF16),
+                vmem((4, TX, COLS), BF16),
                 vmem((2, 3, PL, COLS), BF16),
                 vmem((8, COLS, 128), BF16),
                 vmem((TX, COLS), F32),
@@ -361,7 +385,8 @@
                 dma((2,)), dma((2,)),
                 dma((NT,)), dma((NT,)),
                 dma((2,)), dma((2,)),
-                dma((NT,)), dma((NT,)),
+                dma((4,)), dma((4,)),
+                dma((4,)), dma((4,)),
                 dma((2, 8)), dma((2, 8)),
                 dma, dma,
                 dma((NT,)), dma((NT,)),

time: 41.8 us -> 44.9 us (1.074)
  Pallas kernels: 39.3 us -> 42.5 us
    pallas_call x1, Pallas kernels: 38.6 us -> 41.8 us  [on_device(): pl.pallas_call(functools.partial(kernel, ns), out_shape=(jax.ShapeDtypeSt...]
where the time goes in v5:
time: 44.9 us; the launch traced here: 44.8 us
  Pallas kernels  42.5 us (95%)
  local copies, waits for them, and re-layouts  1.62 us (4%)
  between operations  0.65 us (1%)
    pallas_call x1, Pallas kernels, on_device(): pl.pallas_call(functools.partial(kernel, ns), out_shape=(jax.ShapeDtypeSt...  41.8 us
    unnamed x4, local copies, waits for them, and re-layouts  1.62 us

profile of v5, /device:TPU:57, one launch (start us, length us, event | category | flops | bytes accessed | tf_op | source)
XLA Modules:
  0.0 44.8 jit_solution(9509531935608661921)
XLA Ops:
  0.6 0.0 copy-start.1
  0.6 0.7 %copy-done.1 = s32[2,3,1,1]{1,3,2,0:T(1,128)S(1)} copy-done((s32[2,3,1,1]{1,3,2,0:T(1,128)S(1)}, s32[2,3,1,1]{1,3,2,0:T(1,128)}, u32[]{:S(2)}) %copy-start.1) | copy-done | bytes 48
  1.3 0.0 copy-start
  1.3 0.9 %copy-done = bf16[1,32,4096]{2,1,0:T(8,128)(2,1)S(1)} copy-done((bf16[1,32,4096]{2,1,0:T(8,128)(2,1)S(1)}, bf16[1,32,4096]{2,1,0:T(8,128)(2,1)}, u32[]{:S(2)}) %copy-start) | copy-done | bytes 262168
  2.3 41.8 %shard_map.49 = (f32[2,1,1,512]{3,2,1,0:T(1,128)S(1)}, bf16[1,32,4096]{2,1,0:T(8,128)(2,1)S(1)}, f32[32,256]{1,0:T(8,128)S(1)}) custom-call(bf16[1,32,4096]{2,1,0:T(8,128)(2,1)S(1)} %copy-done, s32[2,1,1,3]{3,2,1,0:T(1,128)S(1)} %bitcast.3), custom_call_target="tpu_custom_call" | custom-call | tf_op jit(solution)/shard_map/pallas_call | solution.py:351
  44.0 0.7 %shard_map.50 = (f32[2,1,1,512]{3,2,1,0:T(1,128)}, bf16[1,32,4096]{2,1,0:T(8,128)(2,1)}, f32[32,256]{1,0:T(8,128)}) custom-call(f32[2,1,1,512]{3,2,1,0:T(1,128)S(1)} %get-tuple-element.6.refs_0_, bf16[1,32,4096]{2,1,0:T(8,128)(2,1)S(1)} %get-tuple-element.7.refs_1_, f32[32,256]{1,0:T(8,128)S(1)} %get-tuple-element.8.refs_2_), custom_call_target="tpu_custom_call" | custom-call | tf_op jit(solution)/shard_map/pallas_call | solution.py:398
Async XLA Ops:
  0.6 0.7 %copy-start.1 = (s32[2,3,1,1]{1,3,2,0:T(1,128)S(1)}, s32[2,3,1,1]{1,3,2,0:T(1,128)}, u32[]{:S(2)}) copy-start(s32[2,3,1,1]{1,3,2,0:T(1,128)} %param.3) | copy-start | bytes 76
  1.3 0.9 %copy-start = (bf16[1,32,4096]{2,1,0:T(8,128)(2,1)S(1)}, bf16[1,32,4096]{2,1,0:T(8,128)(2,1)}, u32[]{:S(2)}) copy-start(bf16[1,32,4096]{2,1,0:T(8,128)(2,1)} %vol_ref.1) | copy-start | bytes 786436

commit v6 on v5

--- a/solution.py
+++ b/solution.py
@@ -39,10 +39,10 @@
 
 def kernel(
     ns, vol_ref, shift_ref, corr_ref, reg_ref, tmpl_ref,
-    edge_out, edge, raw, across, planes, xw, cur, got, sums, shares, win, turned, mean_out,
+    edge_out, edge, raw, across, planes, xw, cur, got, sums, shares, rest, rests, win, turned, mean_out,
     lagged, part, gath,
     local_sem, halo_send, halo_recv, raw_send, raw_recv, rim_send, rim_recv,
-    cur_send, cur_recv, share_send, share_recv, win_send, win_recv, mean_send, mean_recv, part_send, part_recv,
+    cur_send, cur_recv, share_send, share_recv, rest_send, rest_recv, win_send, win_recv, mean_send, mean_recv, part_send, part_recv,
 ):
     t = lax.axis_index("tm")
     s = lax.axis_index("space")
@@ -88,6 +88,39 @@
                     barrier, inc=1, device_id=(beside(dt), s + ds), device_id_type=MESH
                 )
 
+    def source_of(col, half):
+        margin = jnp.where(col < 48, -EDGE, TX) + (col & 7)
+        return jnp.where(col < TX, col, jnp.where((col & 15) >> 3 == half, margin, 2 * PL))
+
+    a = lax.broadcasted_iota(I32, (COLS, COLS), 0)
+    b = lax.broadcasted_iota(I32, (COLS, COLS), 1)
+
+    def plane_tables(i):
+        third = band(shift_ref[i, 0, 0, 2], (b & 63) - (a & 63))
+        for d in range(4):
+            second = band(shift_ref[i, 0, 0, 1], (b >> 6) - (a >> 6) - 4 * (d - 2))
+            planes[i, d] = (second * third).astype(BF16)
+
+    def in_planes(i, n):
+        total = jnp.dot(xw[0 : NT * n], planes[i, 0], preferred_element_type=F32)
+        for d in range(1, 4):
+            total += jnp.dot(
+                xw[d * n : (d + NT) * n], planes[i, d], preferred_element_type=F32
+            )
+        return total.astype(BF16)
+
+    plane_tables(0)
+    row = lax.broadcasted_iota(I32, (TX, TX), 0)
+    col = lax.broadcasted_iota(I32, (TX, TX), 1)
+    from_own = band(shift_ref[0, 0, 0, 0], row - col).astype(BF16)
+    xw[0:64] = jnp.zeros((64, COLS), BF16)
+    xw[18 * TX : 19 * TX] = jnp.zeros((TX, COLS), BF16)
+    for c in range(NT):
+        xw[(c + 2) * TX : (c + 3) * TX] = jnp.dot(
+            from_own, vol_ref[0, :, c * COLS : (c + 1) * COLS], preferred_element_type=F32
+        ).astype(BF16)
+    cur[...] = in_planes(0, TX).reshape(NT, TX, COLS)
+
     for k in range(2):
         wide = vol_ref[0, HALO * k : HALO * k + HALO].astype(F32)[EDGE * k : EDGE * k + EDGE]
         edge_out[k] = jnp.concatenate([wide[:, :HALF], wide[:, HALF:]], axis=0).astype(BF16)
@@ -106,29 +139,21 @@
             raw_send.at[k], raw_recv.at[k], (to, s),
         )
 
+    def cur_copy(k):
+        to = lax.rem(x + k, 4)
+        return remote(
+            cur.at[pl.ds(4 * to, 4)], got.at[x], cur_send.at[k], cur_recv.at[k],
+            (4 * to + z, s),
+        )
+
     for ds in (-1, 1):
         pl.when(there[ds])(halo(ds).start)
+    for k in (2, 1, 3):
+        cur_copy(k).start()
     each_peer(lambda k: raw_copy(k).start())
+    got[x] = cur[pl.ds(4 * x, 4)]
     raw[t, HALO : HALO + TX] = vol_ref[0, :, columns(t)]
 
-    row = lax.broadcasted_iota(I32, (TX, PL), 0)
-    col = lax.broadcasted_iota(I32, (TX, PL), 1)
-    which = (col & 15) >> 3
-    margin = jnp.where(col < 48, -EDGE, TX) + (col & 7)
-    source = [
-        jnp.where(col < TX, col, jnp.where(which == half, margin, 2 * PL)) for half in range(2)
-    ]
-    a = lax.broadcasted_iota(I32, (COLS, COLS), 0)
-    b = lax.broadcasted_iota(I32, (COLS, COLS), 1)
-    for i in range(2):
-        for half in range(2):
-            across[i, half] = band(shift_ref[i, 0, 0, 0], row - source[half]).astype(BF16)
-        third = band(shift_ref[i, 0, 0, 2], (b & 63) - (a & 63))
-        for d in range(4):
-            second = band(shift_ref[i, 0, 0, 1], (b >> 6) - (a >> 6) - 4 * (d - 2))
-            planes[i, d] = (second * third).astype(BF16)
-    xw[0:64] = jnp.zeros((64, COLS), BF16)
-    xw[18 * TX : 19 * TX] = jnp.zeros((TX, COLS), BF16)
     for k, ds, at in ((0, -1, 0), (1, 1, 48)):
 
         @pl.when(jnp.logical_not(there[ds]))
@@ -136,36 +161,37 @@
             edge[k] = jnp.zeros((HALO, HALF), BF16)
             raw[:, at : at + HALO] = jnp.zeros((NT, HALO, COLS), BF16)
             win[:, :, at : at + HALO] = jnp.zeros((2, 3, HALO, COLS), BF16)
+
+    row = lax.broadcasted_iota(I32, (TX, PL), 0)
+    col = lax.broadcasted_iota(I32, (TX, PL), 1)
+    for half in range(2):
+        across[half] = band(shift_ref[1, 0, 0, 0], row - source_of(col, half)).astype(BF16)
+    row = lax.broadcasted_iota(I32, (HALO, TX), 0)
+    row = jnp.where(row < EDGE, row, row + HALO)
+    col = lax.broadcasted_iota(I32, (HALO, TX), 1) + TX
+    from_margins = [
+        band(shift_ref[0, 0, 0, 0], row - source_of(col, half)).astype(BF16) for half in range(2)
+    ]
+    plane_tables(1)
     for ds in (-1, 1):
         pl.when(from_side[ds])(halo(ds).wait_recv)
 
-    def warp(i):
-        for c in range(NT):
-            half, at = c // 8, (c % 8) * COLS
-            rows = [vol_ref[0, :, c * COLS : (c + 1) * COLS]]
-            rows += [edge[k, :, at : at + COLS] for k in range(2)]
-            xw[(c + 2) * TX : (c + 3) * TX] = jnp.dot(
-                across[i, half], jnp.concatenate(rows, axis=0), preferred_element_type=F32
-            ).astype(BF16)
-        total = jnp.dot(xw[0 : NT * TX], planes[i, 0], preferred_element_type=F32)
-        for d in range(1, 4):
-            total += jnp.dot(
-                xw[d * TX : (d + NT) * TX], planes[i, d], preferred_element_type=F32
-            )
-        return total.astype(BF16)
-
-    cur[...] = warp(0).reshape(NT, TX, COLS)
-
-    def cur_copy(k):
-        to = lax.rem(x + k, 4)
-        return remote(
-            cur.at[pl.ds(4 * to, 4)], got.at[x], cur_send.at[k], cur_recv.at[k],
-            (4 * to + z, s),
-        )
-
-    for k in (2, 1, 3):
-        cur_copy(k).start()
-    got[x] = cur[pl.ds(4 * x, 4)]
+    for c in range(NT):
+        half, at = c // 8, (c % 8) * COLS
+        rows = jnp.concatenate([edge[k, :, at : at + COLS] for k in range(2)], axis=0)
+        xw[(c + 2) * HALO : (c + 3) * HALO] = jnp.dot(
+            from_margins[half], rows, preferred_element_type=F32
+        ).astype(BF16)
+    xw[18 * HALO : 19 * HALO] = jnp.zeros((HALO, COLS), BF16)
+    rest[...] = in_planes(0, HALO).reshape(NT, HALO, COLS)
+
+    def rest_copy(k):
+        to = peer(k)
+        return remote(rest.at[snake(to)], rests.at[t], rest_send.at[k], rest_recv.at[k], (to, s))
+
+    each_peer(lambda k: rest_copy(k).start())
+    rests[t] = rest[chunk]
+
     for k in (1, 3, 2):
         cur_copy(k).wait_recv()
     sums[...] = jnp.sum(got[...].astype(F32), axis=0).astype(BF16)
@@ -214,13 +240,27 @@
     for ds in (-1, 1):
         pl.when(there[ds])(rim(ds).start)
 
-    second_warp = warp(1)
+    xw[0:64] = jnp.zeros((64, COLS), BF16)
+    xw[18 * TX : 19 * TX] = jnp.zeros((TX, COLS), BF16)
+    for c in range(NT):
+        half, at = c // 8, (c % 8) * COLS
+        rows = [vol_ref[0, :, c * COLS : (c + 1) * COLS]]
+        rows += [edge[k, :, at : at + COLS] for k in range(2)]
+        xw[(c + 2) * TX : (c + 3) * TX] = jnp.dot(
+            across[half], jnp.concatenate(rows, axis=0), preferred_element_type=F32
+        ).astype(BF16)
+    second_warp = in_planes(1, TX)
     for c in range(NT):
         reg_ref[0, :, c * COLS : (c + 1) * COLS] = second_warp[c * TX : (c + 1) * TX]
 
     for k in (1, 3, 2):
         share_copy(k).wait_recv()
-    mean = jnp.sum(shares[...].astype(F32), axis=0) * (1.0 / NT)
+    each_peer(lambda k: rest_copy(k).wait_recv())
+    mean = jnp.sum(shares[...].astype(F32), axis=0)
+    added = jnp.sum(rests[...].astype(F32), axis=0)
+    mean = jnp.concatenate(
+        [mean[0:8] + added[0:8], mean[8:24], mean[24:32] + added[8:16]], axis=0
+    ) * (1.0 / NT)
     windows(1, mean)
     to_place = remote(
         mean_out, tmpl_ref, mean_send, mean_recv, (chunk, s)
@@ -320,6 +360,7 @@
     for k in range(1, 4):
         cur_copy(k).wait_send()
         share_copy(k).wait_send()
+    each_peer(lambda k: rest_copy(k).wait_send())
     for i in range(2):
         for side in range(8):
             win_copy(i, side, "wait_send")
@@ -368,13 +409,15 @@
                 vmem((2, HALO, HALF), BF16),
                 vmem((2, HALO, HALF), BF16),
                 vmem((NT, PL, COLS), BF16),
-                vmem((2, 2, TX, PL), BF16),
+                vmem((2, TX, PL), BF16),
                 vmem((2, 4, COLS, COLS), BF16),
                 vmem(((NT + 3) * TX, COLS), BF16),
                 vmem((NT, TX, COLS), BF16),
                 vmem((4, 4, TX, COLS), BF16),
                 vmem((4, TX, COLS), BF16),
                 vmem((4, TX, COLS), BF16),
+                vmem((NT, HALO, COLS), BF16),
+                vmem((NT, HALO, COLS), BF16),
                 vmem((2, 3, PL, COLS), BF16),
                 vmem((8, COLS, 128), BF16),
                 vmem((TX, COLS), F32),
@@ -387,6 +430,7 @@
                 dma((2,)), dma((2,)),
                 dma((4,)), dma((4,)),
                 dma((4,)), dma((4,)),
+                dma((NT,)), dma((NT,)),
                 dma((2, 8)), dma((2, 8)),
                 dma, dma,
                 dma((NT,)), dma((NT,)),

time: 44.9 us -> 41.1 us (0.915)
  Pallas kernels: 42.5 us -> 38.7 us
    pallas_call x1, Pallas kernels: 41.8 us -> 37.9 us  [on_device(): pl.pallas_call(functools.partial(kernel, ns), out_shape=(jax.ShapeDtypeSt...]
where the time goes in v6:
time: 41.1 us; the launch traced here: 40.9 us
  Pallas kernels  38.7 us (94%)
  local copies, waits for them, and re-layouts  1.62 us (4%)
  between operations  0.65 us (2%)
    pallas_call x1, Pallas kernels, on_device(): pl.pallas_call(functools.partial(kernel, ns), out_shape=(jax.ShapeDtypeSt...  37.9 us
    unnamed x4, local copies, waits for them, and re-layouts  1.62 us

profile of v6, /device:TPU:57, one launch (start us, length us, event | category | flops | bytes accessed | tf_op | source)
XLA Modules:
  0.0 40.9 jit_solution(5391380811383935774)
XLA Ops:
  0.6 0.0 copy-start.1
  0.6 0.7 %copy-done.1 = s32[2,3,1,1]{1,3,2,0:T(1,128)S(1)} copy-done((s32[2,3,1,1]{1,3,2,0:T(1,128)S(1)}, s32[2,3,1,1]{1,3,2,0:T(1,128)}, u32[]{:S(2)}) %copy-start.1) | copy-done | bytes 48
  1.3 0.0 copy-start
  1.3 0.9 %copy-done = bf16[1,32,4096]{2,1,0:T(8,128)(2,1)S(1)} copy-done((bf16[1,32,4096]{2,1,0:T(8,128)(2,1)S(1)}, bf16[1,32,4096]{2,1,0:T(8,128)(2,1)}, u32[]{:S(2)}) %copy-start) | copy-done | bytes 262168
  2.3 37.9 %shard_map.49 = (f32[2,1,1,512]{3,2,1,0:T(1,128)S(1)}, bf16[1,32,4096]{2,1,0:T(8,128)(2,1)S(1)}, f32[32,256]{1,0:T(8,128)S(1)}) custom-call(bf16[1,32,4096]{2,1,0:T(8,128)(2,1)S(1)} %copy-done, s32[2,1,1,3]{3,2,1,0:T(1,128)S(1)} %bitcast.3), custom_call_target="tpu_custom_call" | custom-call | tf_op jit(solution)/shard_map/pallas_call | solution.py:392
  40.2 0.7 %shard_map.50 = (f32[2,1,1,512]{3,2,1,0:T(1,128)}, bf16[1,32,4096]{2,1,0:T(8,128)(2,1)}, f32[32,256]{1,0:T(8,128)}) custom-call(f32[2,1,1,512]{3,2,1,0:T(1,128)S(1)} %get-tuple-element.6.refs_0_, bf16[1,32,4096]{2,1,0:T(8,128)(2,1)S(1)} %get-tuple-element.7.refs_1_, f32[32,256]{1,0:T(8,128)S(1)} %get-tuple-element.8.refs_2_), custom_call_target="tpu_custom_call" | custom-call | tf_op jit(solution)/shard_map/pallas_call | solution.py:442
Async XLA Ops:
  0.6 0.7 %copy-start.1 = (s32[2,3,1,1]{1,3,2,0:T(1,128)S(1)}, s32[2,3,1,1]{1,3,2,0:T(1,128)}, u32[]{:S(2)}) copy-start(s32[2,3,1,1]{1,3,2,0:T(1,128)} %param.3) | copy-start | bytes 76
  1.3 0.9 %copy-start = (bf16[1,32,4096]{2,1,0:T(8,128)(2,1)S(1)}, bf16[1,32,4096]{2,1,0:T(8,128)(2,1)}, u32[]{:S(2)}) copy-start(bf16[1,32,4096]{2,1,0:T(8,128)(2,1)} %vol_ref.1) | copy-start | bytes 786436

commit v7 on v6

--- a/solution.py
+++ b/solution.py
@@ -15,8 +15,8 @@
 HALO = 16
 NT = 16
 COLS = 256
-EDGE = 8
-HALF = PL * PL // 2
+EDGE = 4
+QUARTER = PL * PL // 4
 OFFSETS = (
     (2, 2), (2, 1), (2, 3), (1, 2), (3, 2), (1, 1), (1, 3), (3, 1), (3, 3),
     (0, 2), (0, 1), (0, 3), (2, 0), (1, 0), (3, 0),
@@ -42,7 +42,7 @@
     edge_out, edge, raw, across, planes, xw, cur, got, sums, shares, rest, rests, win, turned, mean_out,
     lagged, part, gath,
     local_sem, halo_send, halo_recv, raw_send, raw_recv, rim_send, rim_recv,
-    cur_send, cur_recv, share_send, share_recv, rest_send, rest_recv, win_send, win_recv, mean_send, mean_recv, part_send, part_recv,
+    cur_send, cur_recv, share_send, share_recv, rest_send, rest_recv, far_send, far_recv, win_send, win_recv, mean_send, mean_recv, part_send, part_recv,
 ):
     t = lax.axis_index("tm")
     s = lax.axis_index("space")
@@ -50,6 +50,9 @@
     has_lo, has_hi = s > 0, s < ns - 1
     there = {-1: has_lo, 1: has_hi}
     from_side = {-1: has_hi, 1: has_lo}
+    below, above = s == ns // 2 - 1, s == ns // 2
+    far = {-1: above, 1: below}
+    from_far = {-1: below, 1: above}
 
     def peer(k):
         dx, dz = OFFSETS[k]
@@ -88,9 +91,18 @@
                     barrier, inc=1, device_id=(beside(dt), s + ds), device_id_type=MESH
                 )
 
-    def source_of(col, half):
-        margin = jnp.where(col < 48, -EDGE, TX) + (col & 7)
-        return jnp.where(col < TX, col, jnp.where((col & 15) >> 3 == half, margin, 2 * PL))
+    for ds in (-1, 1):
+
+        @pl.when(far[ds])
+        def _():
+            for k in range(NT - 1):
+                pl.semaphore_signal(
+                    barrier, inc=1, device_id=(peer(k), s + ds), device_id_type=MESH
+                )
+
+    def source_of(col, part):
+        margin = jnp.where(col < 48, -EDGE, TX) + (col & 3)
+        return jnp.where(col < TX, col, jnp.where((col & 15) >> 2 == part, margin, 2 * PL))
 
     a = lax.broadcasted_iota(I32, (COLS, COLS), 0)
     b = lax.broadcasted_iota(I32, (COLS, COLS), 1)
@@ -101,13 +113,13 @@
             second = band(shift_ref[i, 0, 0, 1], (b >> 6) - (a >> 6) - 4 * (d - 2))
             planes[i, d] = (second * third).astype(BF16)
 
-    def in_planes(i, n):
+    def in_planes(i, n, dtype=BF16):
         total = jnp.dot(xw[0 : NT * n], planes[i, 0], preferred_element_type=F32)
         for d in range(1, 4):
             total += jnp.dot(
                 xw[d * n : (d + NT) * n], planes[i, d], preferred_element_type=F32
             )
-        return total.astype(BF16)
+        return total.astype(dtype)
 
     plane_tables(0)
     row = lax.broadcasted_iota(I32, (TX, TX), 0)
@@ -122,9 +134,16 @@
     cur[...] = in_planes(0, TX).reshape(NT, TX, COLS)
 
     for k in range(2):
-        wide = vol_ref[0, HALO * k : HALO * k + HALO].astype(F32)[EDGE * k : EDGE * k + EDGE]
-        edge_out[k] = jnp.concatenate([wide[:, :HALF], wide[:, HALF:]], axis=0).astype(BF16)
-    pl.semaphore_wait(barrier, NT - 1 + 3 * (has_lo.astype(I32) + has_hi.astype(I32)))
+        wide = vol_ref[0, HALO * k : HALO * k + HALO].astype(F32)[12 * k : 12 * k + EDGE]
+        edge_out[k] = jnp.concatenate(
+            [wide[:, QUARTER * q : QUARTER * q + QUARTER] for q in range(4)], axis=0
+        ).astype(BF16)
+    pl.semaphore_wait(
+        barrier,
+        NT - 1
+        + 3 * (has_lo.astype(I32) + has_hi.astype(I32))
+        + (NT - 1) * (below.astype(I32) + above.astype(I32)),
+    )
 
     def halo(ds):
         k = 0 if ds < 0 else 1
@@ -151,6 +170,24 @@
     for k in (2, 1, 3):
         cur_copy(k).start()
     each_peer(lambda k: raw_copy(k).start())
+
+    def far_copy(k, ds):
+        to = t if k == NT - 1 else peer(k)
+        src, dst = (0, 48) if ds < 0 else (HALO, 0)
+        return remote(
+            vol_ref.at[0, pl.ds(src, HALO), columns(to)], raw.at[t, pl.ds(dst, HALO)],
+            far_send.at[k], far_recv.at[k], (to, s + ds),
+        )
+
+    def each_far(act, where):
+        for ds in (-1, 1):
+
+            @pl.when(where[ds])
+            def _():
+                for k in range(NT):
+                    getattr(far_copy(k, ds), act)()
+
+    each_far("start", far)
     got[x] = cur[pl.ds(4 * x, 4)]
     raw[t, HALO : HALO + TX] = vol_ref[0, :, columns(t)]
 
@@ -158,32 +195,36 @@
 
         @pl.when(jnp.logical_not(there[ds]))
         def _():
-            edge[k] = jnp.zeros((HALO, HALF), BF16)
+            edge[k] = jnp.zeros((HALO, QUARTER), BF16)
             raw[:, at : at + HALO] = jnp.zeros((NT, HALO, COLS), BF16)
             win[:, :, at : at + HALO] = jnp.zeros((2, 3, HALO, COLS), BF16)
 
     row = lax.broadcasted_iota(I32, (TX, PL), 0)
     col = lax.broadcasted_iota(I32, (TX, PL), 1)
-    for half in range(2):
-        across[half] = band(shift_ref[1, 0, 0, 0], row - source_of(col, half)).astype(BF16)
+    for part_of in range(4):
+        across[part_of] = band(
+            shift_ref[1, 0, 0, 0], row - source_of(col, part_of)
+        ).astype(BF16)
     row = lax.broadcasted_iota(I32, (HALO, TX), 0)
-    row = jnp.where(row < EDGE, row, row + HALO)
+    row = jnp.where(row < EDGE, row, jnp.where(row < 8, row + 24, 8 * PL))
     col = lax.broadcasted_iota(I32, (HALO, TX), 1) + TX
     from_margins = [
-        band(shift_ref[0, 0, 0, 0], row - source_of(col, half)).astype(BF16) for half in range(2)
+        band(shift_ref[0, 0, 0, 0], row - source_of(col, part_of)).astype(BF16)
+        for part_of in range(4)
     ]
     plane_tables(1)
     for ds in (-1, 1):
         pl.when(from_side[ds])(halo(ds).wait_recv)
 
     for c in range(NT):
-        half, at = c // 8, (c % 8) * COLS
+        at = (c % 4) * COLS
         rows = jnp.concatenate([edge[k, :, at : at + COLS] for k in range(2)], axis=0)
         xw[(c + 2) * HALO : (c + 3) * HALO] = jnp.dot(
-            from_margins[half], rows, preferred_element_type=F32
+            from_margins[c // 4], rows, preferred_element_type=F32
         ).astype(BF16)
     xw[18 * HALO : 19 * HALO] = jnp.zeros((HALO, COLS), BF16)
-    rest[...] = in_planes(0, HALO).reshape(NT, HALO, COLS)
+    eight = in_planes(0, HALO, F32).reshape(NT, HALO, COLS)[:, 0:8]
+    rest[...] = jnp.concatenate([eight[:, :, :128], eight[:, :, 128:]], axis=1).astype(BF16)
 
     def rest_copy(k):
         to = peer(k)
@@ -237,17 +278,19 @@
             rim_send.at[k], rim_recv.at[k], (t, s + ds),
         )
 
-    for ds in (-1, 1):
-        pl.when(there[ds])(rim(ds).start)
+    near = {ds: there[ds] & jnp.logical_not(far[ds]) for ds in (-1, 1)}
+    from_near = {ds: from_side[ds] & jnp.logical_not(from_far[ds]) for ds in (-1, 1)}
+    for ds in (-1, 1):
+        pl.when(near[ds])(rim(ds).start)
 
     xw[0:64] = jnp.zeros((64, COLS), BF16)
     xw[18 * TX : 19 * TX] = jnp.zeros((TX, COLS), BF16)
     for c in range(NT):
-        half, at = c // 8, (c % 8) * COLS
+        at = (c % 4) * COLS
         rows = [vol_ref[0, :, c * COLS : (c + 1) * COLS]]
         rows += [edge[k, :, at : at + COLS] for k in range(2)]
         xw[(c + 2) * TX : (c + 3) * TX] = jnp.dot(
-            across[half], jnp.concatenate(rows, axis=0), preferred_element_type=F32
+            across[c // 4], jnp.concatenate(rows, axis=0), preferred_element_type=F32
         ).astype(BF16)
     second_warp = in_planes(1, TX)
     for c in range(NT):
@@ -258,8 +301,15 @@
     each_peer(lambda k: rest_copy(k).wait_recv())
     mean = jnp.sum(shares[...].astype(F32), axis=0)
     added = jnp.sum(rests[...].astype(F32), axis=0)
+    added = jnp.concatenate([added[0:8], added[8:16]], axis=1)
+    first = lax.broadcasted_iota(I32, (8, COLS), 0) < EDGE
     mean = jnp.concatenate(
-        [mean[0:8] + added[0:8], mean[8:24], mean[24:32] + added[8:16]], axis=0
+        [
+            mean[0:8] + jnp.where(first, added, 0.0),
+            mean[8:24],
+            mean[24:32] + jnp.where(first, 0.0, added),
+        ],
+        axis=0,
     ) * (1.0 / NT)
     windows(1, mean)
     to_place = remote(
@@ -272,7 +322,8 @@
     pl.when(chunk != t)(to_place.start)
 
     for ds in (-1, 1):
-        pl.when(from_side[ds])(rim(ds).wait_recv)
+        pl.when(from_near[ds])(rim(ds).wait_recv)
+    each_far("wait_recv", from_far)
     for j in range(8):
         rows16 = raw[:, 16 * (j // 2) : 16 * (j // 2) + 16].astype(F32)
         eight = rows16[:, 8 * (j % 2) : 8 * (j % 2) + 8].reshape(NT * 8, COLS)
@@ -355,7 +406,8 @@
     gath[t] = part[t]
     for ds in (-1, 1):
         pl.when(there[ds])(halo(ds).wait_send)
-        pl.when(there[ds])(rim(ds).wait_send)
+        pl.when(near[ds])(rim(ds).wait_send)
+    each_far("wait_send", far)
     each_peer(lambda k: raw_copy(k).wait_send())
     for k in range(1, 4):
         cur_copy(k).wait_send()
@@ -406,18 +458,18 @@
                 pl.BlockSpec(memory_space=pltpu.VMEM),
             ),
             scratch_shapes=[
-                vmem((2, HALO, HALF), BF16),
-                vmem((2, HALO, HALF), BF16),
+                vmem((2, HALO, QUARTER), BF16),
+                vmem((2, HALO, QUARTER), BF16),
                 vmem((NT, PL, COLS), BF16),
-                vmem((2, TX, PL), BF16),
+                vmem((4, TX, PL), BF16),
                 vmem((2, 4, COLS, COLS), BF16),
                 vmem(((NT + 3) * TX, COLS), BF16),
                 vmem((NT, TX, COLS), BF16),
                 vmem((4, 4, TX, COLS), BF16),
                 vmem((4, TX, COLS), BF16),
                 vmem((4, TX, COLS), BF16),
-                vmem((NT, HALO, COLS), BF16),
-                vmem((NT, HALO, COLS), BF16),
+                vmem((NT, HALO, 128), BF16),
+                vmem((NT, HALO, 128), BF16),
                 vmem((2, 3, PL, COLS), BF16),
                 vmem((8, COLS, 128), BF16),
                 vmem((TX, COLS), F32),
@@ -430,6 +482,7 @@
                 dma((2,)), dma((2,)),
                 dma((4,)), dma((4,)),
                 dma((4,)), dma((4,)),
+                dma((NT,)), dma((NT,)),
                 dma((NT,)), dma((NT,)),
                 dma((2, 8)), dma((2, 8)),
                 dma, dma,

time: 41.1 us -> 40.7 us (level)
  Pallas kernels: 38.7 us -> 38.2 us
    pallas_call x1, Pallas kernels: 37.9 us -> 37.5 us  [on_device(): pl.pallas_call(functools.partial(kernel, ns), out_shape=(jax.ShapeDtypeSt...]
where the time goes in v7:
time: 40.7 us; the launch traced here: 40.5 us
  Pallas kernels  38.2 us (94%)
  local copies, waits for them, and re-layouts  1.62 us (4%)
  between operations  0.65 us (2%)
    pallas_call x1, Pallas kernels, on_device(): pl.pallas_call(functools.partial(kernel, ns), out_shape=(jax.ShapeDtypeSt...  37.5 us
    unnamed x4, local copies, waits for them, and re-layouts  1.62 us

profile of v7, /device:TPU:57, one launch (start us, length us, event | category | flops | bytes accessed | tf_op | source)
XLA Modules:
  0.0 40.5 jit_solution(16367507154298270284)
XLA Ops:
  0.6 0.0 copy-start.1
  0.6 0.7 %copy-done.1 = s32[2,3,1,1]{1,3,2,0:T(1,128)S(1)} copy-done((s32[2,3,1,1]{1,3,2,0:T(1,128)S(1)}, s32[2,3,1,1]{1,3,2,0:T(1,128)}, u32[]{:S(2)}) %copy-start.1) | copy-done | bytes 48
  1.3 0.0 copy-start
  1.3 0.9 %copy-done = bf16[1,32,4096]{2,1,0:T(8,128)(2,1)S(1)} copy-done((bf16[1,32,4096]{2,1,0:T(8,128)(2,1)S(1)}, bf16[1,32,4096]{2,1,0:T(8,128)(2,1)}, u32[]{:S(2)}) %copy-start) | copy-done | bytes 262168
  2.3 37.5 %shard_map.49 = (f32[2,1,1,512]{3,2,1,0:T(1,128)S(1)}, bf16[1,32,4096]{2,1,0:T(8,128)(2,1)S(1)}, f32[32,256]{1,0:T(8,128)S(1)}) custom-call(bf16[1,32,4096]{2,1,0:T(8,128)(2,1)S(1)} %copy-done, s32[2,1,1,3]{3,2,1,0:T(1,128)S(1)} %bitcast.3), custom_call_target="tpu_custom_call" | custom-call | tf_op jit(solution)/shard_map/pallas_call | solution.py:444
  39.8 0.7 %shard_map.50 = (f32[2,1,1,512]{3,2,1,0:T(1,128)}, bf16[1,32,4096]{2,1,0:T(8,128)(2,1)}, f32[32,256]{1,0:T(8,128)}) custom-call(f32[2,1,1,512]{3,2,1,0:T(1,128)S(1)} %get-tuple-element.6.refs_0_, bf16[1,32,4096]{2,1,0:T(8,128)(2,1)S(1)} %get-tuple-element.7.refs_1_, f32[32,256]{1,0:T(8,128)S(1)} %get-tuple-element.8.refs_2_), custom_call_target="tpu_custom_call" | custom-call | tf_op jit(solution)/shard_map/pallas_call | solution.py:495
Async XLA Ops:
  0.6 0.7 %copy-start.1 = (s32[2,3,1,1]{1,3,2,0:T(1,128)S(1)}, s32[2,3,1,1]{1,3,2,0:T(1,128)}, u32[]{:S(2)}) copy-start(s32[2,3,1,1]{1,3,2,0:T(1,128)} %param.3) | copy-start | bytes 76
  1.3 0.9 %copy-start = (bf16[1,32,4096]{2,1,0:T(8,128)(2,1)S(1)}, bf16[1,32,4096]{2,1,0:T(8,128)(2,1)}, u32[]{:S(2)}) copy-start(bf16[1,32,4096]{2,1,0:T(8,128)(2,1)} %vol_ref.1) | copy-start | bytes 786436

commit v8 on v7

--- a/solution.py
+++ b/solution.py
@@ -39,10 +39,11 @@
 
 def kernel(
     ns, vol_ref, shift_ref, corr_ref, reg_ref, tmpl_ref,
-    edge_out, edge, raw, across, planes, xw, cur, got, sums, shares, rest, rests, win, turned, mean_out,
+    edge_out, edge, raw, across, planes, xw, cur, got, sums, shares, rest, rests, over, overs, extras, apart, move, moved, far_planes, win, turned, mean_out,
     lagged, part, gath,
     local_sem, halo_send, halo_recv, raw_send, raw_recv, rim_send, rim_recv,
-    cur_send, cur_recv, share_send, share_recv, rest_send, rest_recv, far_send, far_recv, win_send, win_recv, mean_send, mean_recv, part_send, part_recv,
+    cur_send, cur_recv, share_send, share_recv, rest_send, rest_recv, far_send, far_recv, over_send, over_recv, extra_send, extra_recv, move_send, move_recv,
+    win_send, win_recv, mean_send, mean_recv, part_send, part_recv,
 ):
     t = lax.axis_index("tm")
     s = lax.axis_index("space")
@@ -121,6 +122,10 @@
             )
         return total.astype(dtype)
 
+    row = lax.broadcasted_iota(I32, (8, 128), 0)
+    move[...] = jnp.where(
+        row == 0, shift_ref[0, 0, 0, 0], jnp.where(row == 1, shift_ref[0, 0, 0, 1], shift_ref[0, 0, 0, 2])
+    )
     plane_tables(0)
     row = lax.broadcasted_iota(I32, (TX, TX), 0)
     col = lax.broadcasted_iota(I32, (TX, TX), 1)
@@ -167,6 +172,11 @@
 
     for ds in (-1, 1):
         pl.when(there[ds])(halo(ds).start)
+    def move_copy(ds):
+        return remote(move, moved, move_send, move_recv, (t, s + ds))
+
+    for ds in (-1, 1):
+        pl.when(far[ds])(move_copy(ds).start)
     for k in (2, 1, 3):
         cur_copy(k).start()
     each_peer(lambda k: raw_copy(k).start())
@@ -213,6 +223,20 @@
         for part_of in range(4)
     ]
     plane_tables(1)
+    for k in (1, 3, 2):
+        cur_copy(k).wait_recv()
+    sums[...] = jnp.sum(got[...].astype(F32), axis=0).astype(BF16)
+
+    def share_copy(k):
+        to = 4 * x + lax.rem(z + k, 4)
+        return remote(
+            sums.at[snake(to) - 4 * x], shares.at[z], share_send.at[k], share_recv.at[k], (to, s)
+        )
+
+    for k in (2, 1, 3):
+        share_copy(k).start()
+    shares[z] = sums[chunk - 4 * x]
+
     for ds in (-1, 1):
         pl.when(from_side[ds])(halo(ds).wait_recv)
 
@@ -233,19 +257,52 @@
     each_peer(lambda k: rest_copy(k).start())
     rests[t] = rest[chunk]
 
-    for k in (1, 3, 2):
-        cur_copy(k).wait_recv()
-    sums[...] = jnp.sum(got[...].astype(F32), axis=0).astype(BF16)
-
-    def share_copy(k):
-        to = 4 * x + lax.rem(z + k, 4)
-        return remote(
-            sums.at[snake(to) - 4 * x], shares.at[z], share_send.at[k], share_recv.at[k], (to, s)
-        )
-
-    for k in (2, 1, 3):
-        share_copy(k).start()
-    shares[z] = sums[chunk - 4 * x]
+    at_far = below | above
+    m = below.astype(I32)
+
+    def over_copy(k):
+        to = peer(k)
+        return remote(over.at[snake(to)], overs.at[t], over_send.at[k], over_recv.at[k], (to, s))
+
+    @pl.when(at_far)
+    def _():
+        for ds in (-1, 1):
+            pl.when(from_far[ds])(move_copy(ds).wait_recv)
+        shift = [
+            jnp.concatenate([moved[k : k + 1, :]] * 2, axis=1) for k in range(3)
+        ]
+        third = band(shift[2], (b & 63) - (a & 63))
+        for d in range(4):
+            second = band(shift[1], (b >> 6) - (a >> 6) - 4 * (d - 2))
+            far_planes[d] = (second * third).astype(BF16)
+        row = lax.broadcasted_iota(I32, (HALO, TX), 0)
+        col = lax.broadcasted_iota(I32, (HALO, TX), 1)
+        after = jnp.where(row < 4, row + TX, 8 * PL)
+        before = jnp.where((row >= 4) & (row < 8), row - 8, 8 * PL)
+        weight = band(moved[0:1, 0:TX], m * after + (1 - m) * before - col).astype(BF16)
+        for c in range(NT):
+            xw[(c + 2) * HALO : (c + 3) * HALO] = jnp.dot(
+                weight, vol_ref[0, :, c * COLS : (c + 1) * COLS], preferred_element_type=F32
+            ).astype(BF16)
+        total = jnp.dot(xw[0 : NT * HALO], far_planes[0], preferred_element_type=F32)
+        for d in range(1, 4):
+            total += jnp.dot(
+                xw[d * HALO : (d + NT) * HALO], far_planes[d], preferred_element_type=F32
+            )
+        eight = total.reshape(NT, HALO, COLS)[:, 0:8]
+        over[...] = jnp.concatenate([eight[:, :, :128], eight[:, :, 128:]], axis=1).astype(BF16)
+        each_peer(lambda k: over_copy(k).start())
+        overs[t] = over[chunk]
+
+    @pl.when(jnp.logical_not(at_far))
+    def _():
+        extras[...] = jnp.zeros((3, HALO, COLS), BF16)
+
+    def extra_copy(dt):
+        k = (dt + 1) // 2
+        return remote(
+            extras.at[1], extras.at[1 - dt], extra_send.at[k], extra_recv.at[k], (beside(dt), s)
+        )
 
     def win_copy(i, side, act):
         dt, ds = SIDES[side]
@@ -259,8 +316,18 @@
         present = (from_side if act == "wait_recv" else there).get(ds)
         if present is None:
             getattr(copy, act)()
+        elif i == 1 and act == "start":
+            pl.when(present & jnp.logical_not(far[ds]))(copy.start)
         else:
             pl.when(present)(getattr(copy, act))
+
+    def far_win_copy(side):
+        dt, ds = SIDES[side]
+        src, dst = (0, 48) if ds < 0 else (HALO, 0)
+        return remote(
+            apart.at[pl.ds(src, HALO)], win.at[1, 1 - dt, pl.ds(dst, HALO)],
+            win_send.at[1, side], win_recv.at[1, side], (beside(dt), s + ds),
+        )
 
     def windows(i, mean):
         win[i, 1, HALO : HALO + TX] = mean.astype(BF16)
@@ -298,8 +365,16 @@
 
     for k in (1, 3, 2):
         share_copy(k).wait_recv()
+    mean = jnp.sum(shares[...].astype(F32), axis=0)
+
+    @pl.when(at_far)
+    def _():
+        apart[...] = (mean * (1.0 / NT)).astype(BF16)
+        for side in range(8):
+            if SIDES[side][1]:
+                pl.when(far[SIDES[side][1]])(far_win_copy(side).start)
+
     each_peer(lambda k: rest_copy(k).wait_recv())
-    mean = jnp.sum(shares[...].astype(F32), axis=0)
     added = jnp.sum(rests[...].astype(F32), axis=0)
     added = jnp.concatenate([added[0:8], added[8:16]], axis=1)
     first = lax.broadcasted_iota(I32, (8, COLS), 0) < EDGE
@@ -321,6 +396,15 @@
     pl.when(chunk == t)(put_mean.start)
     pl.when(chunk != t)(to_place.start)
 
+    @pl.when(at_far)
+    def _():
+        each_peer(lambda k: over_copy(k).wait_recv())
+        x16 = jnp.sum(overs[...].astype(F32), axis=0) * (1.0 / NT)
+        x8 = jnp.concatenate([x16[0:8], x16[8:16]], axis=1)
+        extras[1] = jnp.concatenate([x8, jnp.zeros_like(x8)], axis=0).astype(BF16)
+        for dt in (-1, 1):
+            extra_copy(dt).start()
+
     for ds in (-1, 1):
         pl.when(from_near[ds])(rim(ds).wait_recv)
     each_far("wait_recv", from_far)
@@ -337,9 +421,19 @@
     pick = (owner == lax.broadcasted_iota(I32, (NT, 128), 0)).astype(BF16)
 
     def correlate(i):
+        windows = [win[i, k].astype(F32) for k in range(3)]
+        if i == 1:
+            mf = m.astype(F32)
+            for k in range(3):
+                x8 = extras[k].astype(F32)[0:8]
+                w = windows[k]
+                windows[k] = jnp.concatenate(
+                    [w[0:8], w[8:16] + (1.0 - mf) * x8, w[16:48], w[48:56] + mf * x8, w[56:64]],
+                    axis=0,
+                )
         blocks = []
         for half in range(6):
-            x = win[i, half // 2, :, 128 * (half % 2) : 128 * (half % 2) + 128].astype(F32)
+            x = windows[half // 2][:, 128 * (half % 2) : 128 * (half % 2) + 128]
             blocks.append(pltpu.roll(x, 3, 0))
 
         def both(x):
@@ -396,6 +490,13 @@
     for i in range(2):
         for side in range(8):
             win_copy(i, side, "wait_recv")
+        if i == 1:
+
+            @pl.when(at_far)
+            def _():
+                for dt in (-1, 1):
+                    extra_copy(dt).wait_recv()
+
         correlate(i)
 
     def part_copy(k):
@@ -408,6 +509,15 @@
         pl.when(there[ds])(halo(ds).wait_send)
         pl.when(near[ds])(rim(ds).wait_send)
     each_far("wait_send", far)
+
+    @pl.when(at_far)
+    def _():
+        each_peer(lambda k: over_copy(k).wait_send())
+        for dt in (-1, 1):
+            extra_copy(dt).wait_send()
+        for ds in (-1, 1):
+            pl.when(far[ds])(move_copy(ds).wait_send)
+
     each_peer(lambda k: raw_copy(k).wait_send())
     for k in range(1, 4):
         cur_copy(k).wait_send()
@@ -470,6 +580,13 @@
                 vmem((4, TX, COLS), BF16),
                 vmem((NT, HALO, 128), BF16),
                 vmem((NT, HALO, 128), BF16),
+                vmem((NT, HALO, 128), BF16),
+                vmem((NT, HALO, 128), BF16),
+                vmem((3, HALO, COLS), BF16),
+                vmem((TX, COLS), BF16),
+                vmem((8, 128), I32),
+                vmem((8, 128), I32),
+                vmem((4, COLS, COLS), BF16),
                 vmem((2, 3, PL, COLS), BF16),
                 vmem((8, COLS, 128), BF16),
                 vmem((TX, COLS), F32),
@@ -484,6 +601,9 @@
                 dma((4,)), dma((4,)),
                 dma((NT,)), dma((NT,)),
                 dma((NT,)), dma((NT,)),
+                dma((NT,)), dma((NT,)),
+                dma((2,)), dma((2,)),
+                dma, dma,
                 dma((2, 8)), dma((2, 8)),
                 dma, dma,
                 dma((NT,)), dma((NT,)),

time: 40.7 us -> 40.2 us (0.988)
    pallas_call x1, Pallas kernels: 37.5 us -> 37 us  [on_device(): pl.pallas_call(functools.partial(kernel, ns), out_shape=(jax.ShapeDtypeSt...]
where the time goes in v8:
time: 40.2 us; the launch traced here: 40 us
  Pallas kernels  37.8 us (94%)
  local copies, waits for them, and re-layouts  1.62 us (4%)
  between operations  0.65 us (2%)
    pallas_call x1, Pallas kernels, on_device(): pl.pallas_call(functools.partial(kernel, ns), out_shape=(jax.ShapeDtypeSt...  37 us
    unnamed x4, local copies, waits for them, and re-layouts  1.62 us

profile of v8, /device:TPU:57, one launch (start us, length us, event | category | flops | bytes accessed | tf_op | source)
XLA Modules:
  0.0 40.0 jit_solution(17610382323654015328)
XLA Ops:
  0.6 0.0 copy-start.1
  0.6 0.7 %copy-done.1 = s32[2,3,1,1]{1,3,2,0:T(1,128)S(1)} copy-done((s32[2,3,1,1]{1,3,2,0:T(1,128)S(1)}, s32[2,3,1,1]{1,3,2,0:T(1,128)}, u32[]{:S(2)}) %copy-start.1) | copy-done | bytes 48
  1.3 0.0 copy-start
  1.3 0.9 %copy-done = bf16[1,32,4096]{2,1,0:T(8,128)(2,1)S(1)} copy-done((bf16[1,32,4096]{2,1,0:T(8,128)(2,1)S(1)}, bf16[1,32,4096]{2,1,0:T(8,128)(2,1)}, u32[]{:S(2)}) %copy-start) | copy-done | bytes 262168
  2.3 37.0 %shard_map.49 = (f32[2,1,1,512]{3,2,1,0:T(1,128)S(1)}, bf16[1,32,4096]{2,1,0:T(8,128)(2,1)S(1)}, f32[32,256]{1,0:T(8,128)S(1)}) custom-call(bf16[1,32,4096]{2,1,0:T(8,128)(2,1)S(1)} %copy-done, s32[2,1,1,3]{3,2,1,0:T(1,128)S(1)} %bitcast.3), custom_call_target="tpu_custom_call" | custom-call | tf_op jit(solution)/shard_map/pallas_call | solution.py:554
  39.3 0.7 %shard_map.50 = (f32[2,1,1,512]{3,2,1,0:T(1,128)}, bf16[1,32,4096]{2,1,0:T(8,128)(2,1)}, f32[32,256]{1,0:T(8,128)}) custom-call(f32[2,1,1,512]{3,2,1,0:T(1,128)S(1)} %get-tuple-element.6.refs_0_, bf16[1,32,4096]{2,1,0:T(8,128)(2,1)S(1)} %get-tuple-element.7.refs_1_, f32[32,256]{1,0:T(8,128)S(1)} %get-tuple-element.8.refs_2_), custom_call_target="tpu_custom_call" | custom-call | tf_op jit(solution)/shard_map/pallas_call | solution.py:615
Async XLA Ops:
  0.6 0.7 %copy-start.1 = (s32[2,3,1,1]{1,3,2,0:T(1,128)S(1)}, s32[2,3,1,1]{1,3,2,0:T(1,128)}, u32[]{:S(2)}) copy-start(s32[2,3,1,1]{1,3,2,0:T(1,128)} %param.3) | copy-start | bytes 76
  1.3 0.9 %copy-start = (bf16[1,32,4096]{2,1,0:T(8,128)(2,1)S(1)}, bf16[1,32,4096]{2,1,0:T(8,128)(2,1)}, u32[]{:S(2)}) copy-start(bf16[1,32,4096]{2,1,0:T(8,128)(2,1)} %vol_ref.1) | copy-start | bytes 786436

commit v9 on v8

--- a/solution.py
+++ b/solution.py
@@ -350,6 +350,17 @@
     for ds in (-1, 1):
         pl.when(near[ds])(rim(ds).start)
 
+    for k in (1, 3, 2):
+        share_copy(k).wait_recv()
+    mean = jnp.sum(shares[...].astype(F32), axis=0)
+
+    @pl.when(at_far)
+    def _():
+        apart[...] = (mean * (1.0 / NT)).astype(BF16)
+        for side in range(8):
+            if SIDES[side][1]:
+                pl.when(far[SIDES[side][1]])(far_win_copy(side).start)
+
     xw[0:64] = jnp.zeros((64, COLS), BF16)
     xw[18 * TX : 19 * TX] = jnp.zeros((TX, COLS), BF16)
     for c in range(NT):
@@ -362,17 +373,6 @@
     second_warp = in_planes(1, TX)
     for c in range(NT):
         reg_ref[0, :, c * COLS : (c + 1) * COLS] = second_warp[c * TX : (c + 1) * TX]
-
-    for k in (1, 3, 2):
-        share_copy(k).wait_recv()
-    mean = jnp.sum(shares[...].astype(F32), axis=0)
-
-    @pl.when(at_far)
-    def _():
-        apart[...] = (mean * (1.0 / NT)).astype(BF16)
-        for side in range(8):
-            if SIDES[side][1]:
-                pl.when(far[SIDES[side][1]])(far_win_copy(side).start)
 
     each_peer(lambda k: rest_copy(k).wait_recv())
     added = jnp.sum(rests[...].astype(F32), axis=0)

time: 40.2 us -> 40.2 us (level)
  no operation moved by 1% of the time
where the time goes in v9:
time: 40.2 us; the launch traced here: 40 us
  Pallas kernels  37.8 us (94%)
  local copies, waits for them, and re-layouts  1.62 us (4%)
  between operations  0.65 us (2%)
    pallas_call x1, Pallas kernels, on_device(): pl.pallas_call(functools.partial(kernel, ns), out_shape=(jax.ShapeDtypeSt...  37 us
    unnamed x4, local copies, waits for them, and re-layouts  1.62 us

profile of v9, /device:TPU:57, one launch (start us, length us, event | category | flops | bytes accessed | tf_op | source)
XLA Modules:
  0.0 40.0 jit_solution(1440078189968925111)
XLA Ops:
  0.6 0.0 copy-start.1
  0.6 0.7 %copy-done.1 = s32[2,3,1,1]{1,3,2,0:T(1,128)S(1)} copy-done((s32[2,3,1,1]{1,3,2,0:T(1,128)S(1)}, s32[2,3,1,1]{1,3,2,0:T(1,128)}, u32[]{:S(2)}) %copy-start.1) | copy-done | bytes 48
  1.3 0.0 copy-start
  1.3 0.9 %copy-done = bf16[1,32,4096]{2,1,0:T(8,128)(2,1)S(1)} copy-done((bf16[1,32,4096]{2,1,0:T(8,128)(2,1)S(1)}, bf16[1,32,4096]{2,1,0:T(8,128)(2,1)}, u32[]{:S(2)}) %copy-start) | copy-done | bytes 262168
  2.3 37.0 %shard_map.49 = (f32[2,1,1,512]{3,2,1,0:T(1,128)S(1)}, bf16[1,32,4096]{2,1,0:T(8,128)(2,1)S(1)}, f32[32,256]{1,0:T(8,128)S(1)}) custom-call(bf16[1,32,4096]{2,1,0:T(8,128)(2,1)S(1)} %copy-done, s32[2,1,1,3]{3,2,1,0:T(1,128)S(1)} %bitcast.3), custom_call_target="tpu_custom_call" | custom-call | tf_op jit(solution)/shard_map/pallas_call | solution.py:554
  39.3 0.7 %shard_map.50 = (f32[2,1,1,512]{3,2,1,0:T(1,128)}, bf16[1,32,4096]{2,1,0:T(8,128)(2,1)}, f32[32,256]{1,0:T(8,128)}) custom-call(f32[2,1,1,512]{3,2,1,0:T(1,128)S(1)} %get-tuple-element.6.refs_0_, bf16[1,32,4096]{2,1,0:T(8,128)(2,1)S(1)} %get-tuple-element.7.refs_1_, f32[32,256]{1,0:T(8,128)S(1)} %get-tuple-element.8.refs_2_), custom_call_target="tpu_custom_call" | custom-call | tf_op jit(solution)/shard_map/pallas_call | solution.py:615
Async XLA Ops:
  0.6 0.7 %copy-start.1 = (s32[2,3,1,1]{1,3,2,0:T(1,128)S(1)}, s32[2,3,1,1]{1,3,2,0:T(1,128)}, u32[]{:S(2)}) copy-start(s32[2,3,1,1]{1,3,2,0:T(1,128)} %param.3) | copy-start | bytes 76
  1.3 0.9 %copy-start = (bf16[1,32,4096]{2,1,0:T(8,128)(2,1)S(1)}, bf16[1,32,4096]{2,1,0:T(8,128)(2,1)}, u32[]{:S(2)}) copy-start(bf16[1,32,4096]{2,1,0:T(8,128)(2,1)} %vol_ref.1) | copy-start | bytes 786436
